TPU v7x, 32 devices: a whole 2x2x4 slice. The times are simulated.
32 devices in a mesh: seq: 4 (over z), fsdp: 8 (over y, x, core).
Axes of the slice: x: 2, y: 2, z: 4, core: 2. Of those that a mesh axis runs over, the one named last changes fastest.
Arguments:
- tokens: bfloat16 [8, 4096, 1024], P('fsdp', 'seq'), may hold values from -6 to 6
- norm_gain: float32 [1024], replicated, may hold values from 0.25 to 1.75
- in_weight: bfloat16 [1024, 4384], P('fsdp'), may hold values from -0.1875 to 0.1875
- conv_weight: float32 [4, 2304], replicated, may hold values from -3 to 3
- conv_bias: float32 [2304], replicated, may hold values from -3 to 3
- dt_bias: float32 [32], replicated, may hold values from -7 to -2
- a_log: float32 [32], replicated, may hold values from -0.5 to 2.8
- skip_gain: float32 [32], replicated, may hold values from 0.5 to 1.5
- gate_gain: float32 [2048], replicated, may hold values from 0.25 to 1.75
- out_weight: bfloat16 [2048, 1024], P('fsdp'), may hold values from -0.125 to 0.125
- cotangent: bfloat16 [8, 4096, 1024], P('fsdp', 'seq'), may hold values from -6 to 6
Outputs:
- mixed: bfloat16 [8, 4096, 1024], P('fsdp', 'seq')
- grad_tokens: float32 [8, 4096, 1024], P('fsdp', 'seq')
- grad_in_weight: float32 [1024, 4384], P(('seq', 'fsdp'))
- grad_out_weight: float32 [2048, 1024], P(('seq', 'fsdp'))
- grad_norm_gain: float32 [1024], replicated
- grad_conv_weight: float32 [4, 2304], replicated
- grad_conv_bias: float32 [2304], replicated
- grad_dt_bias: float32 [32], replicated
- grad_a_log: float32 [32], replicated
- grad_skip_gain: float32 [32], replicated
- grad_gate_gain: float32 [2048], replicated
All inputs are finite; a program needn't handle non-finite values.
Results may differ from a plain program's by a relative error of at most 0.0088.
Values may be sent and summed in bfloat16 or wider, within the bound.
No kernel may reach another device: no remote copies, remote signals or barrier semaphores. Data moves between devices by JAX's collectives and lax.ppermute only.
A program may use at most 448 MiB of HBM per device.

v0:
```python
import functools

import jax
import jax.numpy as jnp
import ml_dtypes
import numpy as np
from jax import lax
from jax.experimental import pallas as pl
from jax.experimental.pallas import tpu as pltpu
from jax.sharding import PartitionSpec as P

ROWS = 128
GROUP = 2
LANES = 128
HALO = 16
VMEM = 48 * 1024 * 1024
LOG2E = 1.4426950408889634
epsilon = 1e-05
bf16 = jnp.bfloat16
f32 = jnp.float32
highest = lax.Precision.HIGHEST


def shifted(block, axis, distance):
    size = lax.axis_size(axis)
    route = [(i - distance, i) for i in range(size) if 0 <= i - distance < size]
    return lax.ppermute(block, axis, route)


def exchanged(block, axis, bit):
    return lax.ppermute(block, axis, [(i, i ^ bit) for i in range(lax.axis_size(axis))])


def pick(block, at, axis):
    return lax.dynamic_index_in_dim(block, at, axis, keepdims=False)


class Flight:
    def __init__(self, steps):
        self.steps, self.value, self.flying = steps, None, None
        self.advance(None)

    def advance(self, arrived):
        try:
            self.flying = self.steps.send(arrived)
        except StopIteration as end:
            self.flying, self.value = None, end.value

    def step(self, *others):
        if self.flying is not None:
            count = len(self.flying)
            tied = lax.optimization_barrier((*self.flying, *others))
            others = tied[count:]
            self.advance(tuple(tied[:count]))
        return others[0] if len(others) == 1 else others

    def finish(self):
        while self.flying is not None:
            self.advance(self.flying)
        return self.value


def gather(weight):
    rows = weight.shape[0]
    if lax.axis_size("fsdp") != 8 or rows % 32:
        full = lax.all_gather(weight, "fsdp", axis=0, tiled=True)
        return [full[: full.shape[0] // 2]], [full[full.shape[0] // 2 :]]
    first, last = weight[: rows // 2], weight[rows // 2 :]

    def crossed(block):
        return exchanged(block, "fsdp", 1)

    first_y, last_x = exchanged(first, "fsdp", 4), exchanged(last, "fsdp", 2)
    first_x, last_y = exchanged(first, "fsdp", 2), exchanged(last, "fsdp", 4)
    far = [crossed(weight)]
    first_y, last_x, first_x, last_y = yield first_y, last_x, first_x, last_y
    first_xy, last_xy = exchanged(first_y, "fsdp", 2), exchanged(last_x, "fsdp", 4)
    far += [crossed(block) for block in (first_x, last_x, first_y, last_y)]
    first_xy, last_xy, *far = yield first_xy, last_xy, *far
    far += [crossed(first_xy), crossed(last_xy)]
    far = yield tuple(far)
    return [weight, first_x, last_x, first_y, last_y, first_xy, last_xy], list(far)


def gathered_order():
    group = lax.axis_size("fsdp")
    if group != 8:
        return list(range(group))
    me = lax.axis_index("fsdp")
    return [me ^ distance for distance in (0, 2, 4, 6, 1, 3, 5, 7)]


def in_order(block, order):
    size = block.shape[1] // len(order)
    return jnp.concatenate(
        [lax.dynamic_slice_in_dim(block, at * size, size, axis=1) for at in order], axis=1
    )


def handed_on(state, decay, distance):
    entering = jnp.zeros(state.shape, f32)
    state = state.astype(f32)
    for _ in range(lax.axis_size("seq") - 1):
        leaving = (state + decay * entering).astype(bf16)
        (arrived,) = yield (shifted(leaving, "seq", distance),)
        entering = arrived.astype(f32)
    return entering


def sum_all(vector):
    for axis in ("fsdp", "seq"):
        size = lax.axis_size(axis)
        if size & (size - 1):
            vector = lax.psum(vector, axis)
            continue
        for bit in range(size.bit_length() - 1):
            (other,) = yield (exchanged(vector, axis, 1 << bit),)
            vector = vector + other
    return vector


def sum_scatter(parts):
    pieces, group = lax.axis_size("seq"), lax.axis_size("fsdp")
    bits = group.bit_length() - 1
    rows = [part.shape[0] // (pieces * group) for part in parts]
    widths = [part.shape[1] for part in parts]
    fits = len(parts) == 2 and (rows[1] * widths[1]) % widths[0] == 0 or len(parts) == 1 and rows[0] % 2 == 0
    if group != 1 << bits or bits < 1 or not fits:
        return [
            lax.psum_scatter(part.astype(f32), ("seq", "fsdp"), scatter_dimension=0, tiled=True)
            for part in parts
        ]
    me, place = lax.axis_index("fsdp"), lax.axis_index("seq")
    parts = [part.reshape(pieces, group // 2, 2, -1, part.shape[1]) for part in parts]
    mine = me & 1
    got = yield tuple(exchanged(pick(part, 1 - mine, 2), "fsdp", 1) for part in parts)
    halves = [pick(part, mine, 2) + other for part, other in zip(parts, got)]
    if len(halves) == 1:
        halves = [halves[0][:, :, : rows[0] // 2], halves[0][:, :, rows[0] // 2 :]]
    ways = [list(range(bits - 1, 0, -1)), list(range(bits - 1, 0, -1))]
    halves = [part.reshape((pieces,) + (2,) * (bits - 1) + part.shape[2:]) for part in halves]
    for _ in range(bits - 1):
        taken = [ways[0][-1], ways[1][0]]
        places = [1 + ways[way].index(taken[way]) for way in (0, 1)]
        sides = [(me >> taken[way]) & 1 for way in (0, 1)]
        got = yield tuple(
            exchanged(pick(halves[way], 1 - sides[way], places[way]), "fsdp", 1 << taken[way])
            for way in (0, 1)
        )
        halves = [pick(halves[way], sides[way], places[way]) + got[way] for way in (0, 1)]
        for way in (0, 1):
            ways[way].remove(taken[way])
    part = jnp.concatenate([halves[0], halves[1].reshape(pieces, -1, widths[0])], axis=1)
    got = yield tuple(
        lax.ppermute(
            pick(part, (place + ahead) % pieces, 0), "seq", [(i, (i + ahead) % pieces) for i in range(pieces)]
        )
        for ahead in range(1, pieces)
    )
    own = sum((block.astype(f32) for block in got), pick(part, place, 0).astype(f32))
    if len(rows) == 1:
        return [own]
    return [own[: rows[0]], own[rows[0] :].reshape(rows[1], widths[1])]


def mm(a, b):
    return lax.dot_general(a, b, (((1,), (0,)), ((), ())), preferred_element_type=f32)


def mm_nt(a, b):
    return lax.dot_general(a, b, (((1,), (1,)), ((), ())), preferred_element_type=f32)


def mm_tn(a, b):
    return lax.dot_general(a, b, (((0,), (0,)), ((), ())), preferred_element_type=f32)


def sigmoid(v):
    return 0.5 + 0.5 * jnp.tanh(0.5 * v)


def rows_at():
    return lax.broadcasted_iota(jnp.int32, (ROWS, LANES), 0)


def lanes_at():
    return lax.broadcasted_iota(jnp.int32, (ROWS, LANES), 1)


def slab(i):
    return slice(i * LANES, (i + 1) * LANES)


def wide(i):
    return slice(i * 2 * LANES, (i + 1) * 2 * LANES)


def halves(columns, heads):
    lane = lanes_at()
    high = columns.astype(bf16).astype(f32)
    rest = pltpu.roll(columns - high, heads, 1)
    return jnp.where(lane < heads, high, jnp.where(lane < 2 * heads, rest, 0.0)).astype(bf16)


def low_lanes():
    return (lanes_at() < LANES // 2).astype(f32).astype(bf16), (lanes_at() >= LANES // 2).astype(f32).astype(bf16)


def diagonal(block, low, high):
    return jnp.concatenate([block * low, block * high], axis=0)


def parts_of_step():
    return [slice(part * ROWS, (part + 1) * ROWS) for part in range(GROUP)]


def params(**more):
    return pltpu.CompilerParams(vmem_limit_bytes=VMEM, **more)


def cost(microseconds):
    return pl.CostEstimate(flops=int(microseconds * 1e9), bytes_accessed=4 * 1024 * 1024, transcendentals=0)


def whole(shape):
    return pl.BlockSpec(shape, lambda i: (0,) * len(shape))


def by_rows(width, rows=GROUP * ROWS):
    return pl.BlockSpec((rows, width), lambda i: (i, 0))


def conv_kernel(span, rows, pieces, order_ref, before_ref, own_ref, *refs):
    near_refs, far_refs = refs[:pieces], refs[pieces : 2 * pieces]
    taps_ref, bias_ref, act_ref, cin_ref, raw_ref, near_ref, far_ref, held, normed_ref = refs[2 * pieces :]
    at = pl.program_id(0)
    last = pl.num_programs(0) - 1
    near = jnp.concatenate([ref[...] for ref in near_refs], axis=0)
    far = jnp.concatenate([ref[...] for ref in far_refs], axis=0)
    near_ref[...] = near
    far_ref[...] = far
    half = near.shape[0]
    size = own_ref.shape[1] // order_ref.shape[0]

    @pl.when(at == 0)
    def _():
        for i in range(order_ref.shape[0]):
            source = pl.ds(pl.multiple_of(order_ref[i] * size, size), size)
            normed_ref[:HALO, i * size : (i + 1) * size] = before_ref[:, source]
            normed_ref[HALO:, i * size : (i + 1) * size] = own_ref[:, source]

    def projected(start, size):
        block = normed_ref[start : start + size, :]
        return mm(block[:, :half], near) + mm(block[:, half:], far)

    part = 256

    @pl.when(at == last)
    def _():
        for start in range(0, rows, part):
            raw_ref[start : start + part, :] = projected(HALO + start, part)[:, :LANES]

    @pl.when(at < last)
    def _():
        for start, size in [(0, HALO)] + [(HALO + at, part) for at in range(0, rows, part)]:
            block = projected(start, size).astype(bf16)
            cin_ref[start : start + size, :] = block
            held[start : start + size, :] = block.astype(f32)
        for start in range(0, rows, part):
            total = jnp.broadcast_to(bias_ref[0:1, :], (part, bias_ref.shape[1]))
            for k in range(span):
                first = HALO + start - (span - 1) + k
                total = total + taps_ref[k : k + 1, :] * held[first : first + part, :]
            act_ref[start : start + part, :] = (total * sigmoid(total)).astype(bf16)


def conv_forward(order, before, own, near, far, taps, bias):
    rows, width = own.shape
    channels = taps.shape[1]
    total = near[0].shape[1]
    cols = 2 * LANES
    blocks = channels // cols

    def columns(height, upto=blocks):
        return pl.BlockSpec((height, cols), lambda i: (0, jnp.minimum(i, upto)))

    return pl.pallas_call(
        functools.partial(conv_kernel, taps.shape[0], rows, len(near)),
        grid=(blocks + 1,),
        in_specs=[pl.BlockSpec(memory_space=pltpu.SMEM), whole((HALO, width)), whole((rows, width))]
        + [columns(piece.shape[0]) for piece in near + far]
        + [columns(taps.shape[0], blocks - 1), columns(1, blocks - 1)],
        out_specs=[
            columns(rows, blocks - 1),
            columns(rows + HALO, blocks - 1),
            whole((rows, LANES)),
            columns(width // 2),
            columns(width // 2),
        ],
        out_shape=[
            jax.ShapeDtypeStruct((rows, channels), bf16),
            jax.ShapeDtypeStruct((rows + HALO, channels), bf16),
            jax.ShapeDtypeStruct((rows, LANES), f32),
            jax.ShapeDtypeStruct((width // 2, total), bf16),
            jax.ShapeDtypeStruct((width // 2, total), bf16),
        ],
        scratch_shapes=[pltpu.VMEM((rows + HALO, cols), f32), pltpu.VMEM((rows + HALO, width), bf16)],
        compiler_params=params(),
        name="conv_forward",
        cost_estimate=cost(16),
    )(order, before, own, *near, *far, taps, bias)


def steps_kernel(blocks, heads, raw_ref, bias_ref, alog_ref, step_ref, cum_ref, left_ref, right_ref, rows3):
    lane = lanes_at()
    lower = (rows_at() >= lane).astype(f32)
    rates = -jnp.exp(alog_ref[...])
    rows3[...] = jnp.zeros_like(rows3)
    for b in range(blocks):
        rows = slice(b * ROWS, (b + 1) * ROWS)
        soft = raw_ref[rows, :] + bias_ref[...]
        soft = jnp.maximum(soft, 0.0) + jnp.log1p(jnp.exp(-jnp.abs(soft)))
        step = soft.astype(bf16).astype(f32)
        step_ref[rows, :] = step
        cum = jnp.dot(lower, step * rates, precision=highest, preferred_element_type=f32)
        cum_ref[rows, :] = cum
        cum = cum * LOG2E
        parts, rest = [], cum
        for _ in range(3):
            part = rest.astype(bf16).astype(f32)
            parts.append(part)
            rest = rest - part
        left = jnp.where(lane < 3 * heads + 3, 1.0, 0.0)
        for k in (2, 1, 0):
            left = jnp.where(lane < (k + 1) * heads, pltpu.roll(parts[k], k * heads, 1), left)
        left_ref[rows, :] = left.astype(bf16)
        for k in range(3):
            flipped = -parts[k].T
            for h in range(heads):
                rows3[k : k + 1, slab(h)] = flipped[h : h + 1, :]
        right_ref[b * HALO : (b + 1) * HALO, :] = rows3[...].astype(bf16)


def steps_forward(raw, bias, a_log, heads):
    rows = raw.shape[0]
    blocks = rows // ROWS
    shape = jax.ShapeDtypeStruct((rows, LANES), f32)
    return pl.pallas_call(
        functools.partial(steps_kernel, blocks, heads),
        out_shape=[
            shape,
            shape,
            jax.ShapeDtypeStruct((rows, LANES), bf16),
            jax.ShapeDtypeStruct((blocks * HALO, heads * LANES), bf16),
        ],
        scratch_shapes=[pltpu.VMEM((HALO, heads * LANES), f32)],
        compiler_params=params(),
        name="steps_forward",
        cost_estimate=cost(6),
    )(raw, bias, a_log)


def state_kernel(heads, v_ref, b_ref, step_ref, cum_ref, etot_ref, fan_ref, x_ref, f_ref, state, tails, both):
    at = pl.program_id(0)

    @pl.when(at == 0)
    def _():
        state[...] = jnp.zeros_like(state)

    for part, r in enumerate(parts_of_step()):
        cum, step = cum_ref[r, :], step_ref[r, :]
        tail = jnp.exp(cum[ROWS - 1 :, :] - cum) * step
        both[...] = mm(jnp.concatenate([halves(step, heads), halves(tail, heads)], axis=0), fan_ref[...])
        v = v_ref[r, :].astype(f32)
        x_ref[r, :] = (v * both[:ROWS, :]).astype(bf16)
        tails[...] = (v * both[ROWS:, :]).astype(bf16)
        etot = etot_ref[pl.ds(at * GROUP + part, 1), :]
        state[...] = etot * state[...] + mm_tn(b_ref[r, :], tails[...])

    @pl.when(at == pl.num_programs(0) - 1)
    def _():
        f_ref[...] = state[...].astype(bf16)


def piece_state(act, step, cum, etot, fan, heads, inner, width):
    rows = act.shape[0]
    inputs_at = inner // width
    return pl.pallas_call(
        functools.partial(state_kernel, heads),
        grid=(rows // (GROUP * ROWS),),
        in_specs=[
            by_rows(inner),
            pl.BlockSpec((GROUP * ROWS, width), lambda i: (i, inputs_at)),
            by_rows(LANES),
            by_rows(LANES),
            whole(etot.shape),
            whole(fan.shape),
        ],
        out_specs=[by_rows(inner), whole((width, inner))],
        out_shape=[
            jax.ShapeDtypeStruct((rows, inner), bf16),
            jax.ShapeDtypeStruct((width, inner), bf16),
        ],
        scratch_shapes=[
            pltpu.VMEM((width, inner), f32),
            pltpu.VMEM((ROWS, inner), bf16),
            pltpu.VMEM((2 * ROWS, inner), f32),
        ],
        compiler_params=params(),
        name="piece_state",
        cost_estimate=cost(6),
    )(act, act, step, cum, etot, fan)


def inside_kernel(pairs, x_ref, b_ref, c_ref, left_ref, right_ref, still_ref, y_ref, right):
    fixed = left_rows(right, still_ref, right_ref)
    low, high = low_lanes()
    for part, r in enumerate(parts_of_step()):
        scores = jnp.where(rows_at() >= lanes_at(), mm_nt(c_ref[r, :], b_ref[r, :]), 0.0)
        scores = jnp.concatenate([scores, scores], axis=1)
        left = left_ref[r, :]
        for i in range(pairs):
            spread = mm(left, fixed[part, :, wide(i)])
            weights = (scores * jnp.exp2(jnp.minimum(spread, 0.0))).astype(bf16)
            y_ref[r, slab(i)] = mm(weights, diagonal(x_ref[r, slab(i)], low, high))


def left_rows(right, still_ref, right_ref):
    @pl.when(pl.program_id(0) == 0)
    def _():
        for part in range(GROUP):
            right[part, :, :] = still_ref[...]

    own = still_ref.shape[0] - 2 * HALO
    for part in range(GROUP):
        right[part, own : own + HALO, :] = right_ref[part * HALO : (part + 1) * HALO, :]
    return right


def inside_forward(x, act, left, right, still, inner, width):
    rows = act.shape[0]
    inputs_at = inner // width
    return pl.pallas_call(
        functools.partial(inside_kernel, inner // LANES),
        grid=(rows // (GROUP * ROWS),),
        in_specs=[
            by_rows(inner),
            pl.BlockSpec((GROUP * ROWS, width), lambda i: (i, inputs_at)),
            pl.BlockSpec((GROUP * ROWS, width), lambda i: (i, inputs_at + 1)),
            by_rows(LANES),
            by_rows(right.shape[1], GROUP * HALO),
            whole(still.shape),
        ],
        out_specs=by_rows(inner),
        out_shape=jax.ShapeDtypeStruct((rows, inner), f32),
        scratch_shapes=[pltpu.VMEM((GROUP,) + still.shape, bf16)],
        compiler_params=params(),
        name="inside_forward",
        cost_estimate=cost(10),
    )(x, act, act, left, right, still)


def gate_kernel(
    heads,
    pairs,
    y_ref,
    v_ref,
    b_ref,
    c_ref,
    z_ref,
    gn_ref,
    step_ref,
    cum_ref,
    etot_ref,
    ebef_ref,
    skip_ref,
    gain_ref,
    start_ref,
    ones_ref,
    fan_ref,
    out_ref,
    gm_ref,
    gz_ref,
    states_ref,
    pac_ref,
    back_ref,
    ggain_ref,
    gskip_ref,
    state,
    back,
    across,
    mixer,
    gated,
    early,
    tails,
    products,
    both,
):
    at = pl.program_id(0)
    width = pairs * LANES

    @pl.when(at == 0)
    def _():
        state[...] = start_ref[...]
        back[...] = jnp.zeros_like(back)
        ggain_ref[...] = jnp.zeros_like(ggain_ref)
        gskip_ref[...] = jnp.zeros_like(gskip_ref)

    for part, r in enumerate(parts_of_step()):
        outputs = c_ref[r, :]
        entering = state[...].astype(bf16)
        states_ref[part * state.shape[0] : (part + 1) * state.shape[0], :] = entering
        across[...] = mm(outputs, entering)
        cum = cum_ref[r, :]
        grow = jnp.exp(cum)
        tail = jnp.exp(cum[ROWS - 1 :, :] - cum) * step_ref[r, :]
        both[...] = mm(jnp.concatenate([halves(grow, heads), halves(tail, heads)], axis=0), fan_ref[...])
        squares = jnp.zeros((ROWS, LANES), f32)
        meets = jnp.zeros((ROWS, LANES), f32)
        for i in range(pairs):
            s = slab(i)
            v = v_ref[r, s].astype(f32)
            ya = across[:, s] * both[:ROWS, s]
            across[:, s] = ya
            m = (y_ref[r, s] + ya + skip_ref[:, s] * v).astype(bf16)
            mixer[:, s] = m
            z = z_ref[r, s]
            product = m.astype(f32) * (z * sigmoid(z))
            gated[:, s] = product
            squares = squares + product * product
            meets = meets + gn_ref[r, s] * gain_ref[:, s] * product
            tails[:, s] = (v * both[ROWS:, s]).astype(bf16)
        scale = lax.rsqrt(jnp.sum(squares, axis=1, keepdims=True) / width + epsilon)
        pull = scale * scale * scale * (jnp.sum(meets, axis=1, keepdims=True) / width)
        for i in range(pairs):
            s = slab(i)
            v = v_ref[r, s].astype(f32)
            product = gated[:, s]
            unit = product * scale
            gain = gain_ref[:, s]
            gn = gn_ref[r, s]
            out_ref[r, s] = (unit * gain).astype(bf16)
            ggain_ref[:, s] += jnp.sum(gn * unit, axis=0, keepdims=True)
            grad = gn * gain * scale - product * pull
            z = z_ref[r, s]
            sig = sigmoid(z)
            swish = z * sig
            gm = (grad * swish).astype(bf16)
            gm_ref[r, s] = gm
            slope = sig + swish * (1.0 - sig)
            gz_ref[r, s] = (grad * mixer[:, s].astype(f32) * slope).astype(bf16)
            g = gm.astype(f32)
            gskip_ref[:, s] += jnp.sum(g * v, axis=0, keepdims=True)
            products[:, s] = (g * across[:, s]).astype(bf16)
            early[:, s] = (g * both[:ROWS, s]).astype(bf16)
        pac_ref[r, :] = mm(products[...], ones_ref[...])
        block = at * GROUP + part
        back[...] += ebef_ref[pl.ds(block, 1), :] * mm_tn(outputs, early[...])
        state[...] = etot_ref[pl.ds(block, 1), :] * state[...] + mm_tn(b_ref[r, :], tails[...])

    @pl.when(at == pl.num_programs(0) - 1)
    def _():
        back_ref[...] = back[...].astype(bf16)


def gate_both(y, act, z, gn, step, cum, etot, ebef, skip, gain, start, ones, fan, heads, inner, width):
    rows = act.shape[0]
    inputs_at = inner // width
    blocks = rows // ROWS
    return pl.pallas_call(
        functools.partial(gate_kernel, heads, inner // LANES),
        grid=(blocks // GROUP,),
        in_specs=[
            by_rows(inner),
            by_rows(inner),
            pl.BlockSpec((GROUP * ROWS, width), lambda i: (i, inputs_at)),
            pl.BlockSpec((GROUP * ROWS, width), lambda i: (i, inputs_at + 1)),
            by_rows(inner),
            by_rows(inner),
            by_rows(LANES),
            by_rows(LANES),
            whole(etot.shape),
            whole(ebef.shape),
            whole((1, inner)),
            whole((1, inner)),
            whole((width, inner)),
            whole((inner, LANES)),
            whole(fan.shape),
        ],
        out_specs=[
            by_rows(inner),
            by_rows(inner),
            by_rows(inner),
            by_rows(inner, GROUP * width),
            by_rows(LANES),
            whole((width, inner)),
            whole((1, inner)),
            whole((1, inner)),
        ],
        out_shape=[
            jax.ShapeDtypeStruct((rows, inner), bf16),
            jax.ShapeDtypeStruct((rows, inner), bf16),
            jax.ShapeDtypeStruct((rows, inner), bf16),
            jax.ShapeDtypeStruct((blocks * width, inner), bf16),
            jax.ShapeDtypeStruct((rows, LANES), f32),
            jax.ShapeDtypeStruct((width, inner), bf16),
            jax.ShapeDtypeStruct((1, inner), f32),
            jax.ShapeDtypeStruct((1, inner), f32),
        ],
        scratch_shapes=[
            pltpu.VMEM((width, inner), f32),
            pltpu.VMEM((width, inner), f32),
            pltpu.VMEM((ROWS, inner), f32),
            pltpu.VMEM((ROWS, inner), bf16),
            pltpu.VMEM((ROWS, inner), f32),
            pltpu.VMEM((ROWS, inner), bf16),
            pltpu.VMEM((ROWS, inner), bf16),
            pltpu.VMEM((ROWS, inner), bf16),
            pltpu.VMEM((2 * ROWS, inner), f32),
        ],
        compiler_params=params(),
        name="gate_both",
        cost_estimate=cost(18),
    )(y, act, act, act, z, gn, step, cum, etot, ebef, skip, gain, start, ones, fan)


def inside_back_kernel(
    pairs, x_ref, b_ref, c_ref, g_ref, left_ref, right_ref, still_ref, taken_ref,
    dx_ref, db_ref, dc_ref, pq_ref, right, moved, late,
):
    fixed = left_rows(right, still_ref, right_ref)
    lane = lanes_at()
    low, high = low_lanes()
    ones = jnp.ones((16, ROWS), bf16)
    for part, r in enumerate(parts_of_step()):
        inputs, outputs = b_ref[r, :], c_ref[r, :]
        raw_scores = mm_nt(inputs, outputs)
        scores = jnp.where(rows_at() <= lane, raw_scores, 0.0)
        strict = jnp.where(rows_at() < lane, raw_scores, 0.0)
        scores = jnp.concatenate([scores, scores], axis=1)
        strict = jnp.concatenate([strict, strict], axis=1)
        left = -left_ref[r, :]
        gathered = jnp.zeros((ROWS, 2 * LANES), f32)
        for i in range(pairs):
            spread = mm(left, fixed[part, :, wide(i)])
            decay = jnp.exp2(jnp.minimum(spread, 0.0))
            stacked = diagonal(g_ref[r, slab(i)], low, high)
            grad = mm_nt(x_ref[r, slab(i)], stacked) * decay
            gathered = gathered + grad
            moved[:, wide(i)] = (grad * strict).astype(bf16)
            dx_ref[r, slab(i)] = mm((scores * decay).astype(bf16), stacked)
        late[...] = jnp.zeros_like(late)
        for i in range(pairs):
            sums = mm(ones, moved[:, wide(i)])
            late[2 * i : 2 * i + 1, :] = sums[0:1, :LANES]
            late[2 * i + 1 : 2 * i + 2, :] = sums[0:1, LANES:]
        pq_ref[r, :] = late[...].T - mm(moved[...], taken_ref[...])
        gathered = gathered[:, :LANES] + gathered[:, LANES:]
        gathered = jnp.where(rows_at() <= lane, gathered, 0.0).astype(bf16)
        db_ref[r, :] = mm(gathered, outputs)
        dc_ref[r, :] = mm_tn(gathered, inputs)


def inside_backward(x, act, gm, left, right, still, taken, inner, width):
    rows = act.shape[0]
    inputs_at = inner // width
    return pl.pallas_call(
        functools.partial(inside_back_kernel, inner // LANES),
        grid=(rows // (GROUP * ROWS),),
        in_specs=[
            by_rows(inner),
            pl.BlockSpec((GROUP * ROWS, width), lambda i: (i, inputs_at)),
            pl.BlockSpec((GROUP * ROWS, width), lambda i: (i, inputs_at + 1)),
            by_rows(inner),
            by_rows(LANES),
            by_rows(right.shape[1], GROUP * HALO),
            whole(still.shape),
            whole(taken.shape),
        ],
        out_specs=[by_rows(inner), by_rows(width), by_rows(width), by_rows(LANES)],
        out_shape=[
            jax.ShapeDtypeStruct((rows, inner), f32),
            jax.ShapeDtypeStruct((rows, width), f32),
            jax.ShapeDtypeStruct((rows, width), f32),
            jax.ShapeDtypeStruct((rows, LANES), f32),
        ],
        scratch_shapes=[
            pltpu.VMEM((GROUP,) + still.shape, bf16),
            pltpu.VMEM((ROWS, 2 * inner), bf16),
            pltpu.VMEM((LANES, ROWS), f32),
        ],
        compiler_params=params(),
        name="inside_backward",
        cost_estimate=cost(20),
    )(x, act, act, gm, left, right, still, taken)


def finish_kernel(
    heads,
    pairs,
    blocks,
    v_ref,
    x_ref,
    b_ref,
    c_ref,
    g_ref,
    dx_ref,
    db_ref,
    dc_ref,
    pq_ref,
    pac_ref,
    states_ref,
    step_ref,
    cum_ref,
    raw_ref,
    bias_ref,
    alog_ref,
    etot_ref,
    skip_ref,
    start_ref,
    ones_ref,
    fan_ref,
    gact_ref,
    graw_ref,
    gbias_ref,
    grate_ref,
    state,
    tails,
    early,
    first,
    second,
    third,
    spread,
    three,
):
    at = pl.program_id(0)
    step_at = blocks // GROUP - 1 - at
    inner = pairs * LANES
    width = state.shape[0]

    @pl.when(at == 0)
    def _():
        state[...] = start_ref[...]
        gbias_ref[...] = jnp.zeros_like(gbias_ref)
        grate_ref[...] = jnp.zeros_like(grate_ref)

    later = (rows_at() <= lanes_at()).astype(f32)
    earlier = (rows_at() > lanes_at()).astype(f32)
    rates = jnp.exp(alog_ref[...])
    for part, r in reversed(list(enumerate(parts_of_step()))):
        inputs, outputs = b_ref[r, :], c_ref[r, :]
        leaving = state[...]
        leaving_low = leaving.astype(bf16)
        entering = states_ref[part * width : (part + 1) * width, :]
        etot = etot_ref[pl.ds(step_at * GROUP + part, 1), :]
        held = jnp.sum(leaving * entering.astype(f32), axis=0, keepdims=True) * etot
        held = mm(jnp.broadcast_to(held, (8, inner)).astype(bf16), ones_ref[...])[0:1, :]
        spread[...] = mm(inputs, leaving_low)
        cum, step = cum_ref[r, :], step_ref[r, :]
        grow = jnp.exp(cum)
        tail = jnp.exp(cum[ROWS - 1 :, :] - cum)
        three[...] = mm(
            jnp.concatenate([halves(step, heads), halves(tail, heads), halves(grow, heads)], axis=0),
            fan_ref[...],
        )
        for i in range(pairs):
            s = slab(i)
            v = v_ref[r, s].astype(f32)
            g = g_ref[r, s].astype(f32)
            steps = three[:ROWS, s]
            x = x_ref[r, s].astype(f32)
            part_tail = three[ROWS : 2 * ROWS, s]
            more = spread[:, s] * part_tail
            dx = dx_ref[r, s] + more
            first[:, s] = (x * more).astype(bf16)
            direct = v * dx
            high = direct.astype(bf16)
            second[:, s] = high
            third[:, s] = (direct - high.astype(f32)).astype(bf16)
            gact_ref[r, s] = (steps * dx + skip_ref[:, s] * g).astype(bf16)
            tails[:, s] = (x * part_tail).astype(bf16)
            early[:, s] = (g * three[2 * ROWS :, s]).astype(bf16)
        gact_ref[r, inner : inner + width] = (db_ref[r, :] + mm_nt(tails[...], leaving_low)).astype(bf16)
        gact_ref[r, inner + width :] = (dc_ref[r, :] + mm_nt(early[...], entering)).astype(bf16)
        gdecay = (
            jnp.dot(later, pq_ref[r, :] + pac_ref[r, :], precision=highest, preferred_element_type=f32)
            + jnp.dot(
                earlier, mm(first[...], ones_ref[...]), precision=highest, preferred_element_type=f32
            )
            + held
        )
        gstep = mm(second[...], ones_ref[...]) + mm(third[...], ones_ref[...]) - rates * gdecay
        graw = gstep.astype(bf16).astype(f32) * sigmoid(raw_ref[r, :] + bias_ref[...])
        graw_ref[r, :] = graw.astype(bf16)
        gbias_ref[...] += jnp.sum(graw, axis=0, keepdims=True)
        grate_ref[...] += jnp.sum(step * gdecay, axis=0, keepdims=True)
        state[...] = etot * leaving + mm_tn(outputs, early[...])


def mixer_finish(
    act, x, gm, dx, db, dc, pq, pac, states, step, cum, raw, bias, a_log, etot, skip, start, ones, fan, heads, inner, width
):
    rows = act.shape[0]
    blocks = rows // ROWS
    inputs_at = inner // width
    channels = act.shape[1]

    def backwards(columns, height=GROUP * ROWS, column_at=0):
        return pl.BlockSpec((height, columns), lambda i: (blocks // GROUP - 1 - i, column_at))

    return pl.pallas_call(
        functools.partial(finish_kernel, heads, inner // LANES, blocks),
        grid=(blocks // GROUP,),
        in_specs=[
            backwards(inner),
            backwards(inner),
            backwards(width, column_at=inputs_at),
            backwards(width, column_at=inputs_at + 1),
            backwards(inner),
            backwards(inner),
            backwards(width),
            backwards(width),
            backwards(LANES),
            backwards(LANES),
            backwards(inner, GROUP * width),
            backwards(LANES),
            backwards(LANES),
            backwards(LANES),
            whole((1, LANES)),
            whole((1, LANES)),
            whole(etot.shape),
            whole((1, inner)),
            whole((width, inner)),
            whole((inner, LANES)),
            whole(fan.shape),
        ],
        out_specs=[backwards(channels), backwards(LANES), whole((1, LANES)), whole((1, LANES))],
        out_shape=[
            jax.ShapeDtypeStruct((rows, channels), bf16),
            jax.ShapeDtypeStruct((rows, LANES), bf16),
            jax.ShapeDtypeStruct((1, LANES), f32),
            jax.ShapeDtypeStruct((1, LANES), f32),
        ],
        scratch_shapes=[
            pltpu.VMEM((width, inner), f32),
            pltpu.VMEM((ROWS, inner), bf16),
            pltpu.VMEM((ROWS, inner), bf16),
            pltpu.VMEM((ROWS, inner), bf16),
            pltpu.VMEM((ROWS, inner), bf16),
            pltpu.VMEM((ROWS, inner), bf16),
            pltpu.VMEM((ROWS, inner), f32),
            pltpu.VMEM((3 * ROWS, inner), f32),
        ],
        compiler_params=params(),
        name="mixer_finish",
        cost_estimate=cost(16),
    )(act, x, act, act, gm, dx, db, dc, pq, pac, states, step, cum, raw, bias, a_log, etot, skip, start, ones, fan)


def conv_back_kernel(
    span, rows, blocks, cin_ref, gact_ref, graw_ref, taps_ref, bias_ref, next_ref,
    gproj_ref, gtaps_ref, gbias_ref, held, grads,
):
    part = 256
    at = pl.program_id(0)

    @pl.when(at == blocks)
    def _():
        gproj_ref[...] = graw_ref[...]

    @pl.when(at < blocks)
    def _():
        held[...] = cin_ref[...].astype(f32)
        grads[rows : rows + 8, :] = next_ref[...]
        gbias = jnp.zeros((1, LANES), f32)
        gtaps = [jnp.zeros((1, LANES), f32)] * span
        for start in range(0, rows, part):
            total = jnp.broadcast_to(bias_ref[0:1, :], (part, LANES))
            seen = []
            for k in range(span):
                first = HALO + start - (span - 1) + k
                seen.append(held[first : first + part, :])
                total = total + taps_ref[k : k + 1, :] * seen[k]
            sig = sigmoid(total)
            grad = gact_ref[start : start + part, :].astype(f32) * (sig * (1.0 + total * (1.0 - sig)))
            grads[start : start + part, :] = grad
            gbias = gbias + jnp.sum(grad, axis=0, keepdims=True)
            for k in range(span):
                gtaps[k] = gtaps[k] + jnp.sum(seen[k] * grad, axis=0, keepdims=True)
        gbias_ref[...] = gbias
        for k in range(span):
            gtaps_ref[k : k + 1, :] = gtaps[k]
        for start in range(0, rows, part):
            total = jnp.zeros((part, LANES), f32)
            for k in range(span):
                first = start + span - 1 - k
                total = total + taps_ref[k : k + 1, :] * grads[first : first + part, :]
            gproj_ref[start : start + part, :] = total.astype(bf16)


def conv_backward(cin, gact, graw, taps, bias, nexts, begin, blocks, extra):
    rows = gact.shape[0]
    span = taps.shape[0]

    def columns(height, offset=begin):
        return pl.BlockSpec((height, LANES), lambda i: (0, offset + jnp.minimum(i, blocks - 1)))

    return pl.pallas_call(
        functools.partial(conv_back_kernel, span, rows, blocks),
        grid=(blocks + extra,),
        in_specs=[
            columns(rows + HALO),
            columns(rows),
            whole((rows, LANES)),
            columns(span),
            columns(1),
            columns(8),
        ],
        out_specs=[
            pl.BlockSpec((rows, LANES), lambda i: (0, i)),
            columns(span, 0),
            columns(1, 0),
        ],
        out_shape=[
            jax.ShapeDtypeStruct((rows, (blocks + extra) * LANES), bf16),
            jax.ShapeDtypeStruct((span, blocks * LANES), f32),
            jax.ShapeDtypeStruct((1, blocks * LANES), f32),
        ],
        scratch_shapes=[pltpu.VMEM((rows + HALO, LANES), f32), pltpu.VMEM((rows + HALO, LANES), f32)],
        compiler_params=params(),
        name="conv_backward",
        cost_estimate=cost(10),
    )(cin, gact, graw, taps, bias, nexts)


def local(
    tokens,
    norm_gain,
    in_weight,
    conv_weight,
    conv_bias,
    dt_bias,
    a_log,
    skip_gain,
    gate_gain,
    out_weight,
    cotangent,
):
    tokens, incoming = tokens[0], cotangent[0]
    rows, model = tokens.shape
    heads = a_log.shape[0]
    span, channels = conv_weight.shape
    inner = gate_gain.shape[0]
    width = (channels - inner) // 2
    head_width = inner // heads
    blocks = rows // ROWS
    pad = LANES - heads

    order = gathered_order()
    conv_flight = Flight(gather(jnp.pad(in_weight[:, inner:], ((0, 0), (0, pad)))))
    before = shifted(tokens[rows - HALO :], "seq", 1)

    def first_norm(block):
        block = block.astype(f32)
        scale = lax.rsqrt(jnp.mean(block * block, axis=1, keepdims=True) + epsilon)
        return (block * scale * norm_gain).astype(bf16), scale

    own, own_scale = first_norm(tokens)
    gate_part, out_weight, own = conv_flight.step(in_weight[:, :inner], out_weight, own)
    w_gate = lax.all_gather(gate_part, "fsdp", axis=0, tiled=True)
    w_out = lax.all_gather(out_weight, "fsdp", axis=0, tiled=True)
    conv_near, conv_far = conv_flight.finish()
    act, cin, raw, conv_near, conv_far = conv_forward(
        jnp.stack([jnp.int32(at) for at in order]), first_norm(before)[0], own, conv_near, conv_far,
        conv_weight, conv_bias[None],
    )
    bias_row = jnp.pad(dt_bias, (0, pad))[None]
    alog_row = jnp.pad(a_log, (0, pad))[None]
    step, cum, left, right = steps_forward(raw, bias_row, alog_row, heads)

    totals = cum.reshape(blocks, ROWS, LANES)[:, -1, :heads]
    befores = jnp.cumsum(totals, axis=0) - totals
    etot = jnp.repeat(jnp.exp(totals), head_width, axis=1)
    ebef = jnp.repeat(jnp.exp(befores), head_width, axis=1)
    skip = jnp.repeat(skip_gain, head_width)[None]
    def fanned(count, each):
        row, column = np.arange(LANES)[:, None], np.arange(count)[None]
        return ((row < 3 * heads) & (row % heads == column // each)).astype(ml_dtypes.bfloat16)

    def gathering(count, each):
        return (np.arange(count)[:, None] // each == np.arange(LANES)[None]).astype(ml_dtypes.bfloat16)

    fan = fanned(inner, head_width)
    still = fanned(heads * LANES, LANES)
    ones = gathering(inner, head_width)
    taken = gathering(heads * LANES, LANES)
    whole_decay = jnp.repeat(jnp.exp(jnp.sum(totals, axis=0)), head_width)[None]

    x, leaves = piece_state(act, step, cum, etot, fan, heads, inner, width)
    ahead = Flight(handed_on(leaves, whole_decay, 1))
    y = inside_forward(x, act, left, right, still, inner, width)
    y = ahead.step(y)
    z = mm(own, w_gate)
    z = ahead.step(z)
    gn = mm_nt(incoming, w_out)
    gn = ahead.step(gn)
    start = ahead.finish()
    out_in, gm, gz, states, pac, back, ggain, gskip = gate_both(
        y, act, z, gn, step, cum, etot, ebef, skip, gate_gain[None], start, ones, fan, heads, inner, width
    )

    behind = Flight(handed_on(back, whole_decay, -1))
    part_out = mm_tn(out_in, incoming).astype(bf16)
    part_gate = mm_tn(own, gz).astype(bf16)
    pulled_gate = mm_nt(gz, w_gate)
    part_out, part_gate, pulled_gate = behind.step(part_out, part_gate, pulled_gate)
    sums = Flight(sum_scatter([part_out, part_gate]))
    gm = behind.step(gm)
    gm = sums.step(gm)
    dx, db, dc, pq = inside_backward(x, act, gm, left, right, still, taken, inner, width)
    dx = behind.step(dx)
    dx = sums.step(dx)
    back_start = behind.finish()
    gact, graw, gdt, grate = mixer_finish(
        act, x, gm, dx, db, dc, pq, pac, states, step, cum, raw, bias_row, alog_row, etot, skip,
        back_start, ones, fan, heads, inner, width,
    )
    top = conv_bias + jnp.zeros((8, channels), f32)
    for k in range(span):
        first = HALO - (span - 1) + k
        top = top + conv_weight[k] * cin[first : first + 8].astype(f32)
    sig = sigmoid(top)
    nexts = shifted(gact[:8].astype(f32) * (sig * (1.0 + top * (1.0 - sig))), "seq", -1)
    gproj, gtaps, gcbias = conv_backward(
        cin, gact, graw, conv_weight, conv_bias[None], nexts, 0, channels // LANES, 1
    )
    gproj = sums.step(gproj)
    part_conv = mm_tn(own, gproj).astype(bf16)
    conv_sums = Flight(sum_scatter([part_conv]))
    pulled_near = mm_nt(gproj, conv_near)
    pulled_near = conv_sums.step(pulled_near)
    pulled_far = mm_nt(gproj, conv_far)
    pulled_conv = jnp.concatenate([pulled_near, pulled_far], axis=1)
    places = [sum(jnp.where(at == block, i, 0) for i, at in enumerate(order)) for block in range(len(order))]
    grad_normed = pulled_gate + in_order(pulled_conv, places)
    unit = tokens.astype(f32) * own_scale
    pulled = grad_normed * norm_gain
    mean_pull = jnp.mean(pulled * unit, axis=1, keepdims=True)
    grad_tokens = incoming.astype(f32) + own_scale * (pulled - unit * mean_pull)
    grad_norm_gain = jnp.sum(grad_normed * unit, axis=0)
    small = [
        grad_norm_gain,
        gtaps.reshape(-1),
        gcbias[0],
        gdt[0, :heads],
        grate[0, :heads] * -jnp.exp(a_log),
        jnp.sum(gskip.reshape(heads, head_width), axis=1),
        ggain[0],
    ]
    small_sums = Flight(sum_all(jnp.concatenate(small)))
    small_sums.step()
    small_sums.flying = (conv_sums.step(*small_sums.flying),)
    small_sums.step()
    mixed = (tokens.astype(f32) + mm(out_in, w_out)).astype(bf16)
    mixed = conv_sums.step(mixed)
    mixed = sums.step(mixed)
    grad_out_weight, grad_gate_weight = sums.finish()
    (grad_conv_part,) = conv_sums.finish()
    summed = small_sums.finish()

    grad_in_weight = jnp.concatenate(
        [grad_gate_weight, grad_conv_part[:, : channels + heads]], axis=1
    )
    sizes = [part.shape[0] for part in small]
    split, at = [], 0
    for size in sizes:
        split.append(summed[at : at + size])
        at += size
    return (
        mixed[None],
        grad_tokens[None],
        grad_in_weight,
        grad_out_weight,
        split[0],
        split[1].reshape(span, channels),
        *split[2:],
    )


def solution(mesh):
    tokens = P("fsdp", "seq", None)
    sharded = P("fsdp", None)
    spread = P(("seq", "fsdp"), None)
    return jax.shard_map(
        local,
        mesh=mesh,
        in_specs=(tokens, P(), sharded, P(), P(), P(), P(), P(), P(), sharded, tokens),
        out_specs=(tokens, tokens, spread, spread, P(), P(), P(), P(), P(), P(), P()),
        check_vma=False,
    )
```

profile of v0, /device:TPU:0, one launch (start us, length us, event | category | flops | bytes accessed | tf_op | source)
XLA Modules:
  0.0 400.9 jit_solution(4003018994572902426)
XLA Ops:
  21.4 5.9 %collective-permute-done.2.refs_2_ = bf16[64,2432]{1,0:T(8,128)(2,1)S(1)} collective-permute-done((bf16[64,2432]{1,0:T(8,128)(2,1)S(1)}, bf16[64,2432]{1,0:T(8,128)(2,1)S(1)}, u32[]{:S(2)}, u32[]{:S(2)}) %collective-permute-start.2) | collective-permute-done | bytes 311328 | tf_op jit(solution)/shard_map/ppermute | solution.py:31
  36.5 6.6 %collective-permute-done.5.refs_5_ = bf16[64,2432]{1,0:T(8,128)(2,1)S(1)} collective-permute-done((bf16[64,2432]{1,0:T(8,128)(2,1)S(1)}, bf16[64,2432]{1,0:T(8,128)(2,1)S(1)}, u32[]{:S(2)}, u32[]{:S(2)}) %collective-permute-start.5) | collective-permute-done | bytes 311328 | tf_op jit(solution)/shard_map/ppermute | solution.py:31
  43.2 4.7 %collective-permute-done.6.refs_6_ = bf16[64,2432]{1,0:T(8,128)(2,1)S(1)} collective-permute-done((bf16[64,2432]{1,0:T(8,128)(2,1)S(1)}, bf16[64,2432]{1,0:T(8,128)(2,1)S(1)}, u32[]{:S(2)}, u32[]{:S(2)}) %collective-permute-start.6) | collective-permute-done | bytes 311328 | tf_op jit(solution)/shard_map/ppermute | solution.py:31
  50.4 23.4 %conv_forward.1 = (bf16[1024,2304]{1,0:T(8,128)(2,1)}, bf16[1040,2304]{1,0:T(8,128)(2,1)}, f32[1024,128]{1,0:T(8,128)S(1)}, bf16[512,2432]{1,0:T(8,128)(2,1)}, bf16[512,2432]{1,0:T(8,128)(2,1)}) custom-call(s32[8]{0:T(128)S(1)} %stack.35.order_ref, bf16[16,1024]{1,0:T(8,128)(2,1)S(1)} %fusion.59.before_ref, bf16[1024,1024]{1,0:T(8,128)(2,1)} %fusion.4.own_ref, ...), custom_call_target="tpu_custom_call" | custom-call | flops 16000000000 | bytes 4194304 | tf_op jit(solution)/shard_map/conv_forward/pallas_call | solution.py:287
  77.2 7.5 %piece_state.1 = (bf16[1024,2048]{1,0:T(8,128)(2,1)}, bf16[128,2048]{1,0:T(8,128)(2,1)S(1)}) custom-call(bf16[1024,2304]{1,0:T(8,128)(2,1)} %get-tuple-element.88.v_ref.b_ref.c_ref, bf16[1024,2304]{1,0:T(8,128)(2,1)} %get-tuple-element.88.v_ref.b_ref.c_ref, f32[1024,128]{1,0:T(8,128)S(1)} %get-tuple-element.90.step_ref, ...), custom_call_target="tpu_custom_call" | custom-call | flops 6000000000 | bytes 4194304 | tf_op jit(solution)/shard_map/piece_state/pallas_call | solution.py:388
  91.6 9.2 %inside_forward.1.y_ref = f32[1024,2048]{1,0:T(8,128)} custom-call(bf16[1024,2048]{1,0:T(8,128)(2,1)} %get-tuple-element.93.x_ref, bf16[1024,2304]{1,0:T(8,128)(2,1)} %get-tuple-element.88.v_ref.b_ref.c_ref, bf16[1024,2304]{1,0:T(8,128)(2,1)} %get-tuple-element.88.v_ref.b_ref.c_ref, bf16[1024,128]{1,0:T(8,128)(2,1)S(1)} %copy-done.14, ...), custom_call_target="tpu_custom_call" | custom-call | flops 10000000000 | bytes 4194304 | tf_op jit(solution)/shard_map/inside_forward/pallas_call | solution.py:443
  101.9 15.2 %collective-permute-start.15 = (bf16[128,2048]{1,0:T(8,128)(2,1)}, bf16[128,2048]{1,0:T(8,128)(2,1)S(1)}, u32[]{:S(2)}, u32[]{:S(2)}) collective-permute-start(bf16[128,2048]{1,0:T(8,128)(2,1)} %fusion.16), channel_id=1, source_target_pairs={{0,8},{8,16},{16,24},{1,9},{9,17},{17,25},{2,10},{10,18},{18,26},{... | collective-permute-start | bytes 1572872 | tf_op jit(solution)/shard_map/ppermute | solution.py:27
  117.2 10.7 %fusion.63.z_ref = f32[1024,2048]{1,0:T(8,128)} fusion(bf16[1024,1024]{1,0:T(8,128)(2,1)} %fusion.4.own_ref, bf16[1024,2048]{0,1:T(8,128)(2,1)} %all-gather.3.cloned.1.call-done), kind=kOutput, calls=%fused_computation.155 | convolution fusion | flops 4294967296 | bytes 14680064 | tf_op jit(solution)/shard_map/dot_general | solution.py:167
  132.6 10.7 %convolution_bitcast_fusion.gn_ref = f32[1024,2048]{1,0:T(8,128)} fusion(bf16[2048,1024]{1,0:T(8,128)(2,1)} %all-gather.5.cloned.1.call-done, bf16[1,1024,1024]{2,1,0:T(8,128)(2,1)} %param.25), kind=kOutput, calls=%fused_computation.24 | convolution fusion | flops 4294967296 | bytes 14680064 | tf_op jit(solution)/shard_map/dot_general | solution.py:171
  144.5 28.6 %gate_both.1 = (bf16[1024,2048]{1,0:T(8,128)(2,1)}, bf16[1024,2048]{1,0:T(8,128)(2,1)}, bf16[1024,2048]{1,0:T(8,128)(2,1)}, bf16[1024,2048]{1,0:T(8,128)(2,1)}, ...) custom-call(f32[1024,2048]{1,0:T(8,128)} %inside_forward.1.y_ref, ...), custom_call_target="tpu_custom_call" | custom-call | flops 17999998976 | bytes 4194304 | tf_op jit(solution)/shard_map/gate_both/pallas_call | solution.py:570
  173.1 7.2 %convolution_convert_fusion.1 = bf16[1024,2048]{1,0:T(8,128)(2,1)S(1)} fusion(bf16[1024,1024]{1,0:T(8,128)(2,1)S(1)} %copy-done.36, bf16[1024,2048]{1,0:T(8,128)(2,1)} %get-tuple-element.106), kind=kOutput, calls=%fused_computation.34 | convolution fusion | flops 4297064448 | bytes 10485760 | tf_op jit(solution)/shard_map/dot_general | solution.py:175
  182.3 6.1 %fusion.64 = f32[1024,1024]{1,0:T(8,128)} fusion(bf16[1024,2048]{1,0:T(8,128)(2,1)S(1)} %copy-done.57, bf16[1024,2048]{0,1:T(8,128)(2,1)S(1)} %copy-done.55), kind=kOutput, calls=%fused_computation.156 | convolution fusion | flops 4294967296 | bytes 12582912 | tf_op jit(solution)/shard_map/dot_general | solution.py:171
  188.4 4.8 %convolution_convert_fusion.2 = bf16[2048,1024]{1,0:T(8,128)(2,1)S(1)} fusion(bf16[1024,2048]{1,0:T(8,128)(2,1)S(1)} %copy-done.59, bf16[1,1024,1024]{2,1,0:T(8,128)(2,1)S(1)} %copy-done.34), kind=kOutput, calls=%fused_computation.35 | convolution fusion | flops 4297064448 | bytes 10485760 | tf_op jit(solution)/shard_map/dot_general | solution.py:175
  201.6 5.7 %fusion.12 = bf16[1024,1024]{1,0:T(8,128)(2,1)} fusion(bf16[1,1024,1024]{2,1,0:T(8,128)(2,1)S(1)} %copy-done.20, bf16[1024,2048]{1,0:T(8,128)(2,1)S(1)} %copy-done.59, bf16[2048,1024]{1,0:T(8,128)(2,1)S(1)} %copy-done.56), kind=kOutput, calls=%fused_computation.33 | convolution fusion | flops 4298113024 | bytes 12582912 | tf_op jit(solution)/shard_map/dot_general | solution.py:167
  208.6 7.6 %collective-permute-done.20 = bf16[128,2048]{1,0:T(8,128)(2,1)} collective-permute-done((bf16[128,2048]{1,0:T(8,128)(2,1)}, bf16[128,2048]{1,0:T(8,128)(2,1)}, u32[]{:S(2)}, u32[]{:S(2)}) %collective-permute-start.20) | collective-permute-done | bytes 524320 | tf_op jit(solution)/shard_map/ppermute | solution.py:27
  227.0 21.1 %inside_backward.1 = (f32[1024,2048]{1,0:T(8,128)}, f32[1024,128]{1,0:T(8,128)S(1)}, f32[1024,128]{1,0:T(8,128)S(1)}, f32[1024,128]{1,0:T(8,128)S(1)}) custom-call(bf16[1024,2048]{1,0:T(8,128)(2,1)} %get-tuple-element.93.x_ref, bf16[1024,2304]{1,0:T(8,128)(2,1)} %get-tuple-element.88.v_ref.b_ref.c_ref, ...), custom_call_target="tpu_custom_call" | custom-call | flops 20000000000 | bytes 4194304 | tf_op jit(solution)/shard_map/inside_backward/pallas_call | solution.py:667
  251.3 23.0 %mixer_finish.1 = (bf16[1024,2304]{1,0:T(8,128)(2,1)}, bf16[1024,128]{1,0:T(8,128)(2,1)S(1)}, f32[1,128]{1,0:T(1,128)S(1)}, f32[1,128]{1,0:T(1,128)S(1)}) custom-call(bf16[1024,2304]{1,0:T(8,128)(2,1)} %get-tuple-element.88.v_ref.b_ref.c_ref, bf16[1024,2048]{1,0:T(8,128)(2,1)} %get-tuple-element.93.x_ref, ...), custom_call_target="tpu_custom_call" | custom-call | flops 16000000000 | bytes 4194304 | tf_op jit(solution)/shard_map/mixer_finish/pallas_call | solution.py:811
  282.8 18.1 %conv_backward.1 = (bf16[1024,2432]{1,0:T(8,128)(2,1)}, f32[4,2304]{1,0:T(4,128)S(1)}, f32[1,2304]{1,0:T(1,128)S(1)}) custom-call(bf16[1040,2304]{1,0:T(8,128)(2,1)} %get-tuple-element.120.cin_ref, bf16[1024,2304]{1,0:T(8,128)(2,1)S(1)} %copy-done.1, bf16[1024,128]{1,0:T(8,128)(2,1)S(1)} %get-tuple-element.129.graw_ref, f32[4,2304]{1,0:T(4,128)S(1)} %copy-done, ...), custom_call_target="tpu_custom_call" | custom-call | flops 10000000000 | bytes 4194304 | tf_op jit(solution)/shard_map/conv_backward/pallas_call | solution.py:908
  301.0 8.5 %convolution_convert_fusion = bf16[1024,2432]{1,0:T(8,128)(2,1)S(1)} fusion(bf16[1024,1024]{1,0:T(8,128)(2,1)S(1)} %copy-done.37, bf16[1024,2432]{1,0:T(8,128)(2,1)} %get-tuple-element.133), kind=kOutput, calls=%fused_computation.23 | convolution fusion | flops 5102764032 | bytes 12058624 | tf_op jit(solution)/shard_map/dot_general | solution.py:175
  314.2 5.7 %fusion.66 = f32[1024,512]{1,0:T(8,128)S(1)} fusion(bf16[1024,2432]{1,0:T(8,128)(2,1)} %get-tuple-element.133, bf16[512,2432]{1,0:T(8,128)(2,1)} %get-tuple-element.138), kind=kOutput, calls=%fused_computation.158 | convolution fusion | flops 2550136832 | bytes 9568256 | tf_op jit(solution)/shard_map/dot_general | solution.py:171
  354.1 5.2 %collective-permute-done.41 = f32[14688]{0:T(1024)S(1)} collective-permute-done((f32[14688]{0:T(1024)S(1)}, f32[14688]{0:T(1024)S(1)}, u32[]{:S(2)}, u32[]{:S(2)}) %collective-permute-start.41) | collective-permute-done | bytes 58784 | tf_op jit(solution)/shard_map/ppermute | solution.py:31
  359.3 4.7 %collective-permute-start.42 = (f32[14688]{0:T(1024)S(1)}, f32[14688]{0:T(1024)S(1)}, u32[]{:S(2)}, u32[]{:S(2)}) collective-permute-start(f32[14688]{0:T(1024)S(1)} %add.518), channel_id=1, source_target_pairs={{0,16},{8,24},{16,0},{24,8},{1,17},{9,25},{17,1},{25,9},{2,18},{10... | collective-permute-start | bytes 176264 | tf_op jit(solution)/shard_map/ppermute | solution.py:31
  366.2 4.5 %fusion.10 = f32[1,1024,1024]{2,1,0:T(8,128)} fusion(bf16[1,1024,1024]{2,1,0:T(8,128)(2,1)S(1)} %copy-done.35, bf16[1,1024,1024]{2,1,0:T(8,128)(2,1)S(1)} %copy-done.21, f32[1024]{0:T(1024)S(1)} %broadcast_multiply_fusion.1, f32[1024]{0:T(1024)S(1)} %copy-done.42, f32[1024]{0:T(1024)S(1)} %copy-done.44, f32[1024,1024]{1,0:T(8,128)} %fusion.64, ...), kind=kLoop, calls=%fused_computation.31 | loop fusion | flops 9437184 | bytes 16789504 | tf_op jit(solution)/shard_map/broadcast_in_dim | solution.py:1081
  388.1 4.8 %collective-permute-done.38 = bf16[32,2432]{1,0:T(8,128)(2,1)S(1)} collective-permute-done((bf16[32,2432]{1,0:T(8,128)(2,1)S(1)}, bf16[32,2432]{1,0:T(8,128)(2,1)S(1)}, u32[]{:S(2)}, u32[]{:S(2)}) %collective-permute-start.38) | collective-permute-done | bytes 155680 | tf_op jit(solution)/shard_map/ppermute | solution.py:155
  (316 shorter events, 135.5 us)
Async XLA Ops:
  7.2 110.0 %all-gather.3.cloned.1.call-start = ((), (), s32[]{:S(2)}) async-start(), calls=%async_computation | async-start | bytes 4718592 | tf_op jit(solution)/shard_map/all_gather | solution.py:970
  11.8 15.5 %collective-permute-start.3 = (bf16[64,2432]{1,0:T(8,128)(2,1)S(1)}, bf16[64,2432]{1,0:T(8,128)(2,1)S(1)}, u32[]{:S(2)}, u32[]{:S(2)}) collective-permute-start(bf16[64,2432]{1,0:T(8,128)(2,1)S(1)} %get-tuple-element.173), channel_id=1, source_target_pairs={{0,2},{1,3},{2,0},{3,1},{4,6},{5,7},{6,4},{7,5},{8,10},{9,11},{10,... | collective-permute-start | bytes 933896 | tf_op jit(solution)/shard_map/ppermute | solution.py:31
  27.3 105.3 %all-gather.5.cloned.1.call-start = ((), (), s32[]{:S(2)}) async-start(), calls=%async_computation.1 | async-start | bytes 4718592 | tf_op jit(solution)/shard_map/all_gather | solution.py:971
  33.1 14.7 %collective-permute-start.10 = (bf16[64,2432]{1,0:T(8,128)(2,1)S(1)}, bf16[64,2432]{1,0:T(8,128)(2,1)S(1)}, u32[]{:S(2)}, u32[]{:S(2)}) collective-permute-start(bf16[64,2432]{1,0:T(8,128)(2,1)S(1)} %collective-permute-done.1.refs_3_), channel_id=1, source_target_pairs={{0,1},{1,0},{2,3},{3,2},{4,5},{5,4},{6,7},{7,6},{8,9},{9,8},{10,11... | collective-permute-start | bytes 933896 | tf_op jit(solution)/shard_map/ppermute | solution.py:31
  33.1 14.7 %collective-permute-start.6 = (bf16[64,2432]{1,0:T(8,128)(2,1)S(1)}, bf16[64,2432]{1,0:T(8,128)(2,1)S(1)}, u32[]{:S(2)}, u32[]{:S(2)}) collective-permute-start(bf16[64,2432]{1,0:T(8,128)(2,1)S(1)} %collective-permute-done.2.refs_2_), channel_id=1, source_target_pairs={{0,4},{1,5},{2,6},{3,7},{4,0},{5,1},{6,2},{7,3},{8,12},{9,13},{10,... | collective-permute-start | bytes 933896 | tf_op jit(solution)/shard_map/ppermute | solution.py:31
  33.6 14.7 %collective-permute-start.9 = (bf16[64,2432]{1,0:T(8,128)(2,1)S(1)}, bf16[64,2432]{1,0:T(8,128)(2,1)S(1)}, u32[]{:S(2)}, u32[]{:S(2)}) collective-permute-start(bf16[64,2432]{1,0:T(8,128)(2,1)S(1)} %collective-permute-done.2.refs_2_), channel_id=1, source_target_pairs={{0,1},{1,0},{2,3},{3,2},{4,5},{5,4},{6,7},{7,6},{8,9},{9,8},{10,11... | collective-permute-start | bytes 933896 | tf_op jit(solution)/shard_map/ppermute | solution.py:31
  85.6 15.4 %collective-permute-start.14 = (bf16[128,2048]{1,0:T(8,128)(2,1)}, bf16[128,2048]{1,0:T(8,128)(2,1)S(1)}, u32[]{:S(2)}, u32[]{:S(2)}) collective-permute-start(bf16[128,2048]{1,0:T(8,128)(2,1)} %fusion.15), channel_id=1, source_target_pairs={{0,8},{8,16},{16,24},{1,9},{9,17},{17,25},{2,10},{10,18},{18,26},{... | collective-permute-start | bytes 1572872 | tf_op jit(solution)/shard_map/ppermute | solution.py:27
  101.9 26.0 %collective-permute-start.15 = (bf16[128,2048]{1,0:T(8,128)(2,1)}, bf16[128,2048]{1,0:T(8,128)(2,1)S(1)}, u32[]{:S(2)}, u32[]{:S(2)}) collective-permute-start(bf16[128,2048]{1,0:T(8,128)(2,1)} %fusion.16), channel_id=1, source_target_pairs={{0,8},{8,16},{16,24},{1,9},{9,17},{17,25},{2,10},{10,18},{18,26},{... | collective-permute-start | bytes 1572872 | tf_op jit(solution)/shard_map/ppermute | solution.py:27
  128.9 14.5 %collective-permute-start.16 = (bf16[128,2048]{1,0:T(8,128)(2,1)}, bf16[128,2048]{1,0:T(8,128)(2,1)S(1)}, u32[]{:S(2)}, u32[]{:S(2)}) collective-permute-start(bf16[128,2048]{1,0:T(8,128)(2,1)} %fusion.17), channel_id=1, source_target_pairs={{0,8},{8,16},{16,24},{1,9},{9,17},{17,25},{2,10},{10,18},{18,26},{... | collective-permute-start | bytes 1572872 | tf_op jit(solution)/shard_map/ppermute | solution.py:27
  180.5 15.0 %collective-permute-start.17 = (bf16[128,2048]{1,0:T(8,128)(2,1)S(1)}, bf16[128,2048]{1,0:T(8,128)(2,1)S(1)}, u32[]{:S(2)}, u32[]{:S(2)}) collective-permute-start(bf16[128,2048]{1,0:T(8,128)(2,1)S(1)} %fusion.18), channel_id=1, source_target_pairs={{8,0},{16,8},{24,16},{9,1},{17,9},{25,17},{10,2},{18,10},{26,18},{... | collective-permute-start | bytes 1572872 | tf_op jit(solution)/shard_map/ppermute | solution.py:27
  197.2 22.8 %collective-permute-start.19 = (bf16[4,4,32,2048]{3,2,1,0:T(8,128)(2,1)}, bf16[4,4,32,2048]{3,2,1,0:T(8,128)(2,1)}, u32[]{:S(2)}, u32[]{:S(2)}) collective-permute-start(bf16[4,4,32,2048]{3,2,1,0:T(8,128)(2,1)} %dynamic-slice_bitcast_fusion.1), channel_id=1, source_target_pairs={{0,1},{1,0},{2,3},{3,2},{4,5},{5,4},{6,7},{7,6},{8,9},{9,8},{10,11... | collective-permute-start | bytes 6291464 | tf_op jit(solution)/shard_map/ppermute | solution.py:31
  198.7 21.3 %collective-permute-start.18 = (bf16[4,4,64,1024]{3,2,1,0:T(8,128)(2,1)}, bf16[4,4,64,1024]{3,2,1,0:T(8,128)(2,1)}, u32[]{:S(2)}, u32[]{:S(2)}) collective-permute-start(bf16[4,4,64,1024]{3,2,1,0:T(8,128)(2,1)} %dynamic-slice_bitcast_fusion.2), channel_id=1, source_target_pairs={{0,1},{1,0},{2,3},{3,2},{4,5},{5,4},{6,7},{7,6},{8,9},{9,8},{10,11... | collective-permute-start | bytes 6291464 | tf_op jit(solution)/shard_map/ppermute | solution.py:31
  200.3 16.0 %collective-permute-start.20 = (bf16[128,2048]{1,0:T(8,128)(2,1)}, bf16[128,2048]{1,0:T(8,128)(2,1)}, u32[]{:S(2)}, u32[]{:S(2)}) collective-permute-start(bf16[128,2048]{1,0:T(8,128)(2,1)} %fusion.19), channel_id=1, source_target_pairs={{8,0},{16,8},{24,16},{9,1},{17,9},{25,17},{10,2},{18,10},{26,18},{... | collective-permute-start | bytes 1572872 | tf_op jit(solution)/shard_map/ppermute | solution.py:27
  218.3 29.9 %collective-permute-start.23 = (bf16[128,2048]{1,0:T(8,128)(2,1)}, bf16[128,2048]{1,0:T(8,128)(2,1)}, u32[]{:S(2)}, u32[]{:S(2)}) collective-permute-start(bf16[128,2048]{1,0:T(8,128)(2,1)} %fusion.20), channel_id=1, source_target_pairs={{8,0},{16,8},{24,16},{9,1},{17,9},{25,17},{10,2},{18,10},{26,18},{... | collective-permute-start | bytes 1572872 | tf_op jit(solution)/shard_map/ppermute | solution.py:27
  223.8 25.5 %collective-permute-start.22 = (bf16[4,2,32,2048]{3,2,0,1:T(8,128)(2,1)}, bf16[4,2,32,2048]{3,2,0,1:T(8,128)(2,1)S(1)}, u32[]{:S(2)}, u32[]{:S(2)}) collective-permute-start(bf16[4,2,32,2048]{3,2,0,1:T(8,128)(2,1)} %bitcast.128), channel_id=1, source_target_pairs={{0,4},{1,5},{2,6},{3,7},{4,0},{5,1},{6,2},{7,3},{8,12},{9,13},{10,... | collective-permute-start | bytes 3145736 | tf_op jit(solution)/shard_map/ppermute | solution.py:31
  226.9 24.3 %collective-permute-start.21 = (bf16[4,2,64,1024]{3,2,1,0:T(8,128)(2,1)S(1)}, bf16[4,2,64,1024]{3,2,1,0:T(8,128)(2,1)S(1)}, u32[]{:S(2)}, u32[]{:S(2)}) collective-permute-start(bf16[4,2,64,1024]{3,2,1,0:T(8,128)(2,1)S(1)} %dynamic-slice_bitcast_fusion.3), channel_id=1, source_target_pairs={{0,2},{1,3},{2,0},{3,1},{4,6},{5,7},{6,4},{7,5},{8,10},{9,11},{10,... | collective-permute-start | bytes 3145736 | tf_op jit(solution)/shard_map/ppermute | solution.py:31
  277.2 23.8 %collective-permute-start.25 = (bf16[4,32,2048]{2,1,0:T(8,128)(2,1)S(1)}, bf16[4,32,2048]{2,1,0:T(8,128)(2,1)S(1)}, u32[]{:S(2)}, u32[]{:S(2)}) collective-permute-start(bf16[4,32,2048]{2,1,0:T(8,128)(2,1)S(1)} %dynamic-slice_bitcast_fusion.6), channel_id=1, source_target_pairs={{0,2},{1,3},{2,0},{3,1},{4,6},{5,7},{6,4},{7,5},{8,10},{9,11},{10,... | collective-permute-start | bytes 1572872 | tf_op jit(solution)/shard_map/ppermute | solution.py:31
  277.7 23.2 %collective-permute-start.24 = (bf16[4,64,1024]{2,1,0:T(8,128)(2,1)S(1)}, bf16[4,64,1024]{2,1,0:T(8,128)(2,1)S(1)}, u32[]{:S(2)}, u32[]{:S(2)}) collective-permute-start(bf16[4,64,1024]{2,1,0:T(8,128)(2,1)S(1)} %dynamic-slice_bitcast_fusion.7), channel_id=1, source_target_pairs={{0,4},{1,5},{2,6},{3,7},{4,0},{5,1},{6,2},{7,3},{8,12},{9,13},{10,... | collective-permute-start | bytes 1572872 | tf_op jit(solution)/shard_map/ppermute | solution.py:31
  326.3 21.2 %collective-permute-start.32 = (bf16[4,2,16,2432]{3,2,1,0:T(8,128)(2,1)}, bf16[4,2,16,2432]{3,2,1,0:T(8,128)(2,1)}, u32[]{:S(2)}, u32[]{:S(2)}) collective-permute-start(bf16[4,2,16,2432]{3,2,1,0:T(8,128)(2,1)} %dynamic-slice_bitcast_fusion.4), channel_id=1, source_target_pairs={{0,4},{1,5},{2,6},{3,7},{4,0},{5,1},{6,2},{7,3},{8,12},{9,13},{10,... | collective-permute-start | bytes 1867784 | tf_op jit(solution)/shard_map/ppermute | solution.py:31
  327.7 19.7 %collective-permute-start.31 = (bf16[4,2,16,2432]{3,2,1,0:T(8,128)(2,1)}, bf16[4,2,16,2432]{3,2,1,0:T(8,128)(2,1)}, u32[]{:S(2)}, u32[]{:S(2)}) collective-permute-start(bf16[4,2,16,2432]{3,2,1,0:T(8,128)(2,1)} %dynamic-slice_bitcast_fusion.5), channel_id=1, source_target_pairs={{0,2},{1,3},{2,0},{3,1},{4,6},{5,7},{6,4},{7,5},{8,10},{9,11},{10,... | collective-permute-start | bytes 1867784 | tf_op jit(solution)/shard_map/ppermute | solution.py:31
  334.9 39.9 %collective-permute-start.27 = (bf16[128,1024]{1,0:T(8,128)(2,1)}, bf16[128,1024]{1,0:T(8,128)(2,1)}, u32[]{:S(2)}, u32[]{:S(2)}) collective-permute-start(bf16[128,1024]{1,0:T(8,128)(2,1)} %get-tuple-element.166), channel_id=1, source_target_pairs={{0,8},{8,16},{16,24},{24,0},{1,9},{9,17},{17,25},{25,1},{2,10},{10... | collective-permute-start | bytes 786440 | tf_op jit(solution)/shard_map/ppermute | solution.py:155
  336.9 37.9 %collective-permute-start.28 = (bf16[128,1024]{1,0:T(8,128)(2,1)}, bf16[128,1024]{1,0:T(8,128)(2,1)}, u32[]{:S(2)}, u32[]{:S(2)}) collective-permute-start(bf16[128,1024]{1,0:T(8,128)(2,1)} %get-tuple-element.167), channel_id=1, source_target_pairs={{0,16},{8,24},{16,0},{24,8},{1,17},{9,25},{17,1},{25,9},{2,18},{10... | collective-permute-start | bytes 786440 | tf_op jit(solution)/shard_map/ppermute | solution.py:155
  344.2 30.6 %collective-permute-start.29 = (bf16[128,1024]{1,0:T(8,128)(2,1)}, bf16[128,1024]{1,0:T(8,128)(2,1)}, u32[]{:S(2)}, u32[]{:S(2)}) collective-permute-start(bf16[128,1024]{1,0:T(8,128)(2,1)} %get-tuple-element.165), channel_id=1, source_target_pairs={{0,24},{8,0},{16,8},{24,16},{1,25},{9,1},{17,9},{25,17},{2,26},{10... | collective-permute-start | bytes 786440 | tf_op jit(solution)/shard_map/ppermute | solution.py:155
  351.9 22.0 %collective-permute-start.36 = (bf16[4,16,2432]{2,1,0:T(8,128)(2,1)}, bf16[4,16,2432]{2,1,0:T(8,128)(2,1)}, u32[]{:S(2)}, u32[]{:S(2)}) collective-permute-start(bf16[4,16,2432]{2,1,0:T(8,128)(2,1)} %dynamic-slice_bitcast_fusion.8), channel_id=1, source_target_pairs={{0,2},{1,3},{2,0},{3,1},{4,6},{5,7},{6,4},{7,5},{8,10},{9,11},{10,... | collective-permute-start | bytes 933896 | tf_op jit(solution)/shard_map/ppermute | solution.py:31
  (85 other events, 897.6 us)
Sparse Core Ops, SparseCore 0:
  27.4 40.7 all-gather.2
  70.1 36.7 all-gather.4
where the time goes:
time: 407 us; the launch traced here: 401 us
  Pallas kernels  132 us (32%)
  starting transfers between devices  65.8 us (16%)
  matrix products  62.4 us (15%)
  waiting for transfers between devices  54.2 us (13%)
  other arithmetic  38.2 us (9%)
  local copies, waits for them, and re-layouts  32.5 us (8%)
  between operations  15.4 us (4%)
    ppermute x29, waiting for transfers between devices, exchanged(): lax.ppermute(block, axis, [(i, i ^ bit) for i in range(lax.axis_size(axis...  32.5 us
    ppermute x8, starting transfers between devices, shifted(): return lax.ppermute(block, axis, route)  32.2 us
    pallas_call x1, Pallas kernels, gate_both(): pl.pallas_call(functools.partial(gate_kernel, heads, inner // LANES), gri...  28.6 us
    dot_general x4, matrix products, mm_nt(): lax.dot_general(a, b, (((1,), (1,)), ((), ())), preferred_element_type=f32)  25.5 us
    pallas_call x1, Pallas kernels, conv_forward(): pl.pallas_call(functools.partial(conv_kernel, taps.shape[0], rows, len(ne...  23.4 us
    pallas_call x1, Pallas kernels, mixer_finish(): pl.pallas_call(functools.partial(finish_kernel, heads, inner // LANES, bl...  23 us
    pallas_call x1, Pallas kernels, inside_backward(): pl.pallas_call(functools.partial(inside_back_kernel, inner // LANES), gri...  21.1 us
    dot_general x3, matrix products, mm_tn(): lax.dot_general(a, b, (((0,), (0,)), ((), ())), preferred_element_type=f32)  20.5 us
  transfers between devices with their start and end apart: 45, of which 17 were waited for; matrix products, arithmetic and copies ran while one was open for 23% of the time, Pallas kernels for 20%

commit v1 on v0

--- a/solution.py
+++ b/solution.py
@@ -73,13 +73,11 @@
     first_y, last_x = exchanged(first, "fsdp", 4), exchanged(last, "fsdp", 2)
     first_x, last_y = exchanged(first, "fsdp", 2), exchanged(last, "fsdp", 4)
     far = [crossed(weight)]
-    first_y, last_x, first_x, last_y = yield first_y, last_x, first_x, last_y
     first_xy, last_xy = exchanged(first_y, "fsdp", 2), exchanged(last_x, "fsdp", 4)
     far += [crossed(block) for block in (first_x, last_x, first_y, last_y)]
-    first_xy, last_xy, *far = yield first_xy, last_xy, *far
+    first_xy, last_xy = yield first_xy, last_xy
     far += [crossed(first_xy), crossed(last_xy)]
-    far = yield tuple(far)
-    return [weight, first_x, last_x, first_y, last_y, first_xy, last_xy], list(far)
+    return [weight, first_x, last_x, first_y, last_y, first_xy, last_xy], far
 
 
 def gathered_order():
@@ -257,12 +255,12 @@
 
     @pl.when(at == last)
     def _():
-        for start in range(0, rows, part):
-            raw_ref[start : start + part, :] = projected(HALO + start, part)[:, :LANES]
+        for start in range(0, rows, rows // 2):
+            raw_ref[start : start + rows // 2, :] = projected(HALO + start, rows // 2)[:, :LANES]
 
     @pl.when(at < last)
     def _():
-        for start, size in [(0, HALO)] + [(HALO + at, part) for at in range(0, rows, part)]:
+        for start, size in [(0, HALO + rows)]:
             block = projected(start, size).astype(bf16)
             cin_ref[start : start + size, :] = block
             held[start : start + size, :] = block.astype(f32)
@@ -966,7 +964,7 @@
         return (block * scale * norm_gain).astype(bf16), scale
 
     own, own_scale = first_norm(tokens)
-    gate_part, out_weight, own = conv_flight.step(in_weight[:, :inner], out_weight, own)
+    gate_part, out_weight = conv_flight.step(in_weight[:, :inner], out_weight)
     w_gate = lax.all_gather(gate_part, "fsdp", axis=0, tiled=True)
     w_out = lax.all_gather(out_weight, "fsdp", axis=0, tiled=True)
     conv_near, conv_far = conv_flight.finish()
@@ -1015,8 +1013,8 @@
     pulled_gate = mm_nt(gz, w_gate)
     part_out, part_gate, pulled_gate = behind.step(part_out, part_gate, pulled_gate)
     sums = Flight(sum_scatter([part_out, part_gate]))
+    gm = sums.step(gm)
     gm = behind.step(gm)
-    gm = sums.step(gm)
     dx, db, dc, pq = inside_backward(x, act, gm, left, right, still, taken, inner, width)
     dx = behind.step(dx)
     dx = sums.step(dx)

time: 407 us -> 407 us (level)
  waiting for transfers between devices: 54.2 us -> 41.4 us
  starting transfers between devices: 65.8 us -> 73.9 us
  matrix products: 62.4 us -> 66.5 us
    ppermute x29, starting transfers between devices: 18.8 us -> 28.3 us  [exchanged(): lax.ppermute(block, axis, [(i, i ^ bit) for i in range(lax.axis_size(axis...]
    ppermute x29, waiting for transfers between devices: 32.5 us -> 25.2 us  [exchanged(): lax.ppermute(block, axis, [(i, i ^ bit) for i in range(lax.axis_size(axis...]
    ppermute x8, waiting for transfers between devices: 14.5 us -> 9.05 us  [shifted(): return lax.ppermute(block, axis, route)]
    dot_general x2, matrix products: 16.4 us -> 20.6 us  [mm(): lax.dot_general(a, b, (((1,), (0,)), ((), ())), preferred_element_type=f32)]
    unnamed x129 -> x121, local copies, waits for them, and re-layouts: 11.1 us -> 12.2 us
  transfers between devices with their start and end apart: 45 -> 45, of which waited for: 17 -> 16; matrix products, arithmetic and copies ran while one was open for 23% -> 24% of each run, Pallas kernels for 20% -> 20%
where the time goes in v1:
time: 407 us; the launch traced here: 402 us
  Pallas kernels  131 us (32%)
  starting transfers between devices  73.9 us (18%)
  matrix products  66.5 us (16%)
  waiting for transfers between devices  41.4 us (10%)
  other arithmetic  41.1 us (10%)
  local copies, waits for them, and re-layouts  32.4 us (8%)
  between operations  15.3 us (4%)
    ppermute x8, starting transfers between devices, shifted(): return lax.ppermute(block, axis, route)  32.4 us
    pallas_call x1, Pallas kernels, gate_both(): pl.pallas_call(functools.partial(gate_kernel, heads, inner // LANES), gri...  28.6 us
    ppermute x29, starting transfers between devices, exchanged(): lax.ppermute(block, axis, [(i, i ^ bit) for i in range(lax.axis_size(axis...  28.3 us
    dot_general x4, matrix products, mm_nt(): lax.dot_general(a, b, (((1,), (1,)), ((), ())), preferred_element_type=f32)  25.5 us
    ppermute x29, waiting for transfers between devices, exchanged(): lax.ppermute(block, axis, [(i, i ^ bit) for i in range(lax.axis_size(axis...  25.2 us
    pallas_call x1, Pallas kernels, mixer_finish(): pl.pallas_call(functools.partial(finish_kernel, heads, inner // LANES, bl...  22.7 us
    pallas_call x1, Pallas kernels, conv_forward(): pl.pallas_call(functools.partial(conv_kernel, taps.shape[0], rows, len(ne...  22.5 us
    pallas_call x1, Pallas kernels, inside_backward(): pl.pallas_call(functools.partial(inside_back_kernel, inner // LANES), gri...  21.1 us
  transfers between devices with their start and end apart: 45, of which 16 were waited for; matrix products, arithmetic and copies ran while one was open for 24% of the time, Pallas kernels for 20%

profile of v1, /device:TPU:0, one launch (start us, length us, event | category | flops | bytes accessed | tf_op | source)
XLA Modules:
  0.0 401.6 jit_solution(11925400131520851422)
XLA Ops:
  14.1 6.1 %collective-permute-done.3.refs_3_ = bf16[64,2432]{1,0:T(8,128)(2,1)S(1)} collective-permute-done((bf16[64,2432]{1,0:T(8,128)(2,1)}, bf16[64,2432]{1,0:T(8,128)(2,1)S(1)}, u32[]{:S(2)}, u32[]{:S(2)}) %collective-permute-start.3) | collective-permute-done | bytes 311328 | tf_op jit(solution)/shard_map/ppermute | solution.py:31
  48.0 22.5 %conv_forward.1 = (bf16[1024,2304]{1,0:T(8,128)(2,1)}, bf16[1040,2304]{1,0:T(8,128)(2,1)}, f32[1024,128]{1,0:T(8,128)S(1)}, bf16[512,2432]{1,0:T(8,128)(2,1)}, bf16[512,2432]{1,0:T(8,128)(2,1)}) custom-call(s32[8]{0:T(128)S(1)} %stack.35.order_ref, bf16[16,1024]{1,0:T(8,128)(2,1)S(1)} %fusion.59.before_ref, bf16[1024,1024]{1,0:T(8,128)(2,1)} %fusion.4.own_ref, ...), custom_call_target="tpu_custom_call" | custom-call | flops 16000000000 | bytes 4194304 | tf_op jit(solution)/shard_map/conv_forward/pallas_call | solution.py:285
  74.0 7.4 %piece_state.1 = (bf16[1024,2048]{1,0:T(8,128)(2,1)}, bf16[128,2048]{1,0:T(8,128)(2,1)S(1)}) custom-call(bf16[1024,2304]{1,0:T(8,128)(2,1)} %get-tuple-element.82.v_ref.b_ref.c_ref, bf16[1024,2304]{1,0:T(8,128)(2,1)} %get-tuple-element.82.v_ref.b_ref.c_ref, f32[1024,128]{1,0:T(8,128)S(1)} %get-tuple-element.84.step_ref, ...), custom_call_target="tpu_custom_call" | custom-call | flops 6000000000 | bytes 4194304 | tf_op jit(solution)/shard_map/piece_state/pallas_call | solution.py:386
  82.3 4.3 %collective-permute-start.14 = (bf16[128,2048]{1,0:T(8,128)(2,1)}, bf16[128,2048]{1,0:T(8,128)(2,1)}, u32[]{:S(2)}, u32[]{:S(2)}) collective-permute-start(bf16[128,2048]{1,0:T(8,128)(2,1)} %fusion.15), channel_id=1, source_target_pairs={{0,8},{8,16},{16,24},{1,9},{9,17},{17,25},{2,10},{10,18},{18,26},{... | collective-permute-start | bytes 1572872 | tf_op jit(solution)/shard_map/ppermute | solution.py:27
  89.0 9.1 %inside_forward.1.y_ref = f32[1024,2048]{1,0:T(8,128)} custom-call(bf16[1024,2048]{1,0:T(8,128)(2,1)} %get-tuple-element.87.x_ref, bf16[1024,2304]{1,0:T(8,128)(2,1)} %get-tuple-element.82.v_ref.b_ref.c_ref, bf16[1024,2304]{1,0:T(8,128)(2,1)} %get-tuple-element.82.v_ref.b_ref.c_ref, bf16[1024,128]{1,0:T(8,128)(2,1)S(1)} %copy-done.14, ...), custom_call_target="tpu_custom_call" | custom-call | flops 10000000000 | bytes 4194304 | tf_op jit(solution)/shard_map/inside_forward/pallas_call | solution.py:441
  100.1 14.9 %collective-permute-start.15 = (bf16[128,2048]{1,0:T(8,128)(2,1)}, bf16[128,2048]{1,0:T(8,128)(2,1)S(1)}, u32[]{:S(2)}, u32[]{:S(2)}) collective-permute-start(bf16[128,2048]{1,0:T(8,128)(2,1)} %fusion.16), channel_id=1, source_target_pairs={{0,8},{8,16},{16,24},{1,9},{9,17},{17,25},{2,10},{10,18},{18,26},{... | collective-permute-start | bytes 1572872 | tf_op jit(solution)/shard_map/ppermute | solution.py:27
  115.0 10.7 %fusion.63.z_ref = f32[1024,2048]{1,0:T(8,128)} fusion(bf16[1024,1024]{1,0:T(8,128)(2,1)} %fusion.4.own_ref, bf16[1024,2048]{0,1:T(8,128)(2,1)} %all-gather.3.cloned.1.call-done), kind=kOutput, calls=%fused_computation.155 | convolution fusion | flops 4294967296 | bytes 14680064 | tf_op jit(solution)/shard_map/dot_general | solution.py:165
  130.3 10.7 %convolution_bitcast_fusion.gn_ref = f32[1024,2048]{1,0:T(8,128)} fusion(bf16[2048,1024]{1,0:T(8,128)(2,1)} %all-gather.5.cloned.1.call-done, bf16[1,1024,1024]{2,1,0:T(8,128)(2,1)} %param.25), kind=kOutput, calls=%fused_computation.24 | convolution fusion | flops 4294967296 | bytes 14680064 | tf_op jit(solution)/shard_map/dot_general | solution.py:169
  142.2 28.6 %gate_both.1 = (bf16[1024,2048]{1,0:T(8,128)(2,1)}, bf16[1024,2048]{1,0:T(8,128)(2,1)}, bf16[1024,2048]{1,0:T(8,128)(2,1)}, bf16[1024,2048]{1,0:T(8,128)(2,1)}, ...) custom-call(f32[1024,2048]{1,0:T(8,128)} %inside_forward.1.y_ref, ...), custom_call_target="tpu_custom_call" | custom-call | flops 17999998976 | bytes 4194304 | tf_op jit(solution)/shard_map/gate_both/pallas_call | solution.py:568
  170.9 7.2 %convolution_convert_fusion.1 = bf16[1024,2048]{1,0:T(8,128)(2,1)S(1)} fusion(bf16[1024,1024]{1,0:T(8,128)(2,1)S(1)} %copy-done.37, bf16[1024,2048]{1,0:T(8,128)(2,1)} %get-tuple-element.100), kind=kOutput, calls=%fused_computation.34 | convolution fusion | flops 4297064448 | bytes 10485760 | tf_op jit(solution)/shard_map/dot_general | solution.py:173
  180.0 6.1 %fusion.64 = f32[1024,1024]{1,0:T(8,128)} fusion(bf16[1024,2048]{1,0:T(8,128)(2,1)S(1)} %copy-done.53, bf16[1024,2048]{0,1:T(8,128)(2,1)S(1)} %copy-done.52), kind=kOutput, calls=%fused_computation.156 | convolution fusion | flops 4294967296 | bytes 12582912 | tf_op jit(solution)/shard_map/dot_general | solution.py:169
  186.2 4.9 %convolution_convert_fusion.2 = bf16[2048,1024]{1,0:T(8,128)(2,1)S(1)} fusion(bf16[1024,2048]{1,0:T(8,128)(2,1)S(1)} %copy-done.55, bf16[1,1024,1024]{2,1,0:T(8,128)(2,1)S(1)} %copy-done.36), kind=kOutput, calls=%fused_computation.35 | convolution fusion | flops 4297064448 | bytes 10485760 | tf_op jit(solution)/shard_map/dot_general | solution.py:173
  200.3 9.9 %fusion.12 = bf16[1024,1024]{1,0:T(8,128)(2,1)} fusion(bf16[1,1024,1024]{2,1,0:T(8,128)(2,1)} %param.15, bf16[1024,2048]{1,0:T(8,128)(2,1)} %get-tuple-element.99, bf16[2048,1024]{1,0:T(8,128)(2,1)} %all-gather.5.cloned.1.call-done), kind=kOutput, calls=%fused_computation.33 | convolution fusion | flops 4298113024 | bytes 12582912 | tf_op jit(solution)/shard_map/dot_general | solution.py:165
  211.6 4.2 %collective-permute-done.22 = bf16[128,2048]{1,0:T(8,128)(2,1)} collective-permute-done((bf16[128,2048]{1,0:T(8,128)(2,1)}, bf16[128,2048]{1,0:T(8,128)(2,1)}, u32[]{:S(2)}, u32[]{:S(2)}) %collective-permute-start.22) | collective-permute-done | bytes 524320 | tf_op jit(solution)/shard_map/ppermute | solution.py:27
  227.8 21.1 %inside_backward.1 = (f32[1024,2048]{1,0:T(8,128)}, f32[1024,128]{1,0:T(8,128)S(1)}, f32[1024,128]{1,0:T(8,128)S(1)}, f32[1024,128]{1,0:T(8,128)S(1)}) custom-call(bf16[1024,2048]{1,0:T(8,128)(2,1)} %get-tuple-element.87.x_ref, bf16[1024,2304]{1,0:T(8,128)(2,1)} %get-tuple-element.82.v_ref.b_ref.c_ref, ...), custom_call_target="tpu_custom_call" | custom-call | flops 20000000000 | bytes 4194304 | tf_op jit(solution)/shard_map/inside_backward/pallas_call | solution.py:665
  251.2 22.7 %mixer_finish.1 = (bf16[1024,2304]{1,0:T(8,128)(2,1)}, bf16[1024,128]{1,0:T(8,128)(2,1)S(1)}, f32[1,128]{1,0:T(1,128)S(1)}, f32[1,128]{1,0:T(1,128)S(1)}) custom-call(bf16[1024,2304]{1,0:T(8,128)(2,1)} %get-tuple-element.82.v_ref.b_ref.c_ref, bf16[1024,2048]{1,0:T(8,128)(2,1)} %get-tuple-element.87.x_ref, ...), custom_call_target="tpu_custom_call" | custom-call | flops 16000000000 | bytes 4194304 | tf_op jit(solution)/shard_map/mixer_finish/pallas_call | solution.py:809
  281.7 18.2 %conv_backward.1 = (bf16[1024,2432]{1,0:T(8,128)(2,1)}, f32[4,2304]{1,0:T(4,128)S(1)}, f32[1,2304]{1,0:T(1,128)S(1)}) custom-call(bf16[1040,2304]{1,0:T(8,128)(2,1)} %get-tuple-element.114.cin_ref, bf16[1024,2304]{1,0:T(8,128)(2,1)S(1)} %copy-done.1, bf16[1024,128]{1,0:T(8,128)(2,1)S(1)} %get-tuple-element.123.graw_ref, f32[4,2304]{1,0:T(4,128)S(1)} %copy-done, ...), custom_call_target="tpu_custom_call" | custom-call | flops 10000000000 | bytes 4194304 | tf_op jit(solution)/shard_map/conv_backward/pallas_call | solution.py:906
  300.6 8.3 %convolution_convert_fusion = bf16[1024,2432]{1,0:T(8,128)(2,1)S(1)} fusion(bf16[1024,1024]{1,0:T(8,128)(2,1)S(1)} %copy-done.38, bf16[1024,2432]{1,0:T(8,128)(2,1)} %get-tuple-element.127), kind=kOutput, calls=%fused_computation.23 | convolution fusion | flops 5102764032 | bytes 12058624 | tf_op jit(solution)/shard_map/dot_general | solution.py:173
  314.7 5.8 %fusion.66 = f32[1024,512]{1,0:T(8,128)S(1)} fusion(bf16[1024,2432]{1,0:T(8,128)(2,1)} %get-tuple-element.127, bf16[512,2432]{1,0:T(8,128)(2,1)} %get-tuple-element.132), kind=kOutput, calls=%fused_computation.158 | convolution fusion | flops 2550136832 | bytes 9568256 | tf_op jit(solution)/shard_map/dot_general | solution.py:169
  341.2 3.8 collective-permute-done.34
  354.9 4.7 %collective-permute-done.41 = f32[14688]{0:T(1024)S(1)} collective-permute-done((f32[14688]{0:T(1024)S(1)}, f32[14688]{0:T(1024)S(1)}, u32[]{:S(2)}, u32[]{:S(2)}) %collective-permute-start.41) | collective-permute-done | bytes 58784 | tf_op jit(solution)/shard_map/ppermute | solution.py:31
  359.6 5.4 %collective-permute-start.42 = (f32[14688]{0:T(1024)S(1)}, f32[14688]{0:T(1024)S(1)}, u32[]{:S(2)}, u32[]{:S(2)}) collective-permute-start(f32[14688]{0:T(1024)S(1)} %add.518), channel_id=1, source_target_pairs={{0,16},{8,24},{16,0},{24,8},{1,17},{9,25},{17,1},{25,9},{2,18},{10... | collective-permute-start | bytes 176264 | tf_op jit(solution)/shard_map/ppermute | solution.py:31
  367.5 5.1 %fusion.10 = f32[1,1024,1024]{2,1,0:T(8,128)} fusion(bf16[1,1024,1024]{2,1,0:T(8,128)(2,1)} %param.25, bf16[1,1024,1024]{2,1,0:T(8,128)(2,1)S(1)} %copy-done.21, f32[1024]{0:T(1024)S(1)} %broadcast_multiply_fusion.1, f32[1024]{0:T(1024)S(1)} %copy-done.43, f32[1024]{0:T(1024)S(1)} %copy-done.45, f32[1024,1024]{1,0:T(8,128)} %fusion.64, ...), kind=kLoop, calls=%fused_computation.31 | loop fusion | flops 9437184 | bytes 16789504 | tf_op jit(solution)/shard_map/broadcast_in_dim | solution.py:1079
  388.9 4.7 %collective-permute-done.38 = bf16[32,2432]{1,0:T(8,128)(2,1)S(1)} collective-permute-done((bf16[32,2432]{1,0:T(8,128)(2,1)S(1)}, bf16[32,2432]{1,0:T(8,128)(2,1)S(1)}, u32[]{:S(2)}, u32[]{:S(2)}) %collective-permute-start.38) | collective-permute-done | bytes 155680 | tf_op jit(solution)/shard_map/ppermute | solution.py:153
  (308 shorter events, 140.0 us)
Async XLA Ops:
  7.2 107.8 %all-gather.3.cloned.1.call-start = ((), (), s32[]{:S(2)}) async-start(), calls=%async_computation | async-start | bytes 4718592 | tf_op jit(solution)/shard_map/all_gather | solution.py:968
  29.9 100.3 %all-gather.5.cloned.1.call-start = ((), (), s32[]{:S(2)}) async-start(), calls=%async_computation.1 | async-start | bytes 4718592 | tf_op jit(solution)/shard_map/all_gather | solution.py:969
  30.0 14.4 %collective-permute-start.4 = (bf16[64,2432]{1,0:T(8,128)(2,1)}, bf16[64,2432]{1,0:T(8,128)(2,1)S(1)}, u32[]{:S(2)}, u32[]{:S(2)}) collective-permute-start(bf16[64,2432]{1,0:T(8,128)(2,1)} %get-tuple-element.166), channel_id=1, source_target_pairs={{0,4},{1,5},{2,6},{3,7},{4,0},{5,1},{6,2},{7,3},{8,12},{9,13},{10,... | collective-permute-start | bytes 933896 | tf_op jit(solution)/shard_map/ppermute | solution.py:31
  31.6 13.3 %collective-permute-start.1 = (bf16[64,2432]{1,0:T(8,128)(2,1)}, bf16[64,2432]{1,0:T(8,128)(2,1)S(1)}, u32[]{:S(2)}, u32[]{:S(2)}) collective-permute-start(bf16[64,2432]{1,0:T(8,128)(2,1)} %get-tuple-element.167), channel_id=1, source_target_pairs={{0,2},{1,3},{2,0},{3,1},{4,6},{5,7},{6,4},{7,5},{8,10},{9,11},{10,... | collective-permute-start | bytes 933896 | tf_op jit(solution)/shard_map/ppermute | solution.py:31
  82.3 15.8 %collective-permute-start.14 = (bf16[128,2048]{1,0:T(8,128)(2,1)}, bf16[128,2048]{1,0:T(8,128)(2,1)}, u32[]{:S(2)}, u32[]{:S(2)}) collective-permute-start(bf16[128,2048]{1,0:T(8,128)(2,1)} %fusion.15), channel_id=1, source_target_pairs={{0,8},{8,16},{16,24},{1,9},{9,17},{17,25},{2,10},{10,18},{18,26},{... | collective-permute-start | bytes 1572872 | tf_op jit(solution)/shard_map/ppermute | solution.py:27
  100.1 25.6 %collective-permute-start.15 = (bf16[128,2048]{1,0:T(8,128)(2,1)}, bf16[128,2048]{1,0:T(8,128)(2,1)S(1)}, u32[]{:S(2)}, u32[]{:S(2)}) collective-permute-start(bf16[128,2048]{1,0:T(8,128)(2,1)} %fusion.16), channel_id=1, source_target_pairs={{0,8},{8,16},{16,24},{1,9},{9,17},{17,25},{2,10},{10,18},{18,26},{... | collective-permute-start | bytes 1572872 | tf_op jit(solution)/shard_map/ppermute | solution.py:27
  126.7 14.4 %collective-permute-start.16 = (bf16[128,2048]{1,0:T(8,128)(2,1)}, bf16[128,2048]{1,0:T(8,128)(2,1)S(1)}, u32[]{:S(2)}, u32[]{:S(2)}) collective-permute-start(bf16[128,2048]{1,0:T(8,128)(2,1)} %fusion.17), channel_id=1, source_target_pairs={{0,8},{8,16},{16,24},{1,9},{9,17},{17,25},{2,10},{10,18},{18,26},{... | collective-permute-start | bytes 1572872 | tf_op jit(solution)/shard_map/ppermute | solution.py:27
  178.3 14.9 %collective-permute-start.17 = (bf16[128,2048]{1,0:T(8,128)(2,1)S(1)}, bf16[128,2048]{1,0:T(8,128)(2,1)S(1)}, u32[]{:S(2)}, u32[]{:S(2)}) collective-permute-start(bf16[128,2048]{1,0:T(8,128)(2,1)S(1)} %fusion.18), channel_id=1, source_target_pairs={{8,0},{16,8},{24,16},{9,1},{17,9},{25,17},{10,2},{18,10},{26,18},{... | collective-permute-start | bytes 1572872 | tf_op jit(solution)/shard_map/ppermute | solution.py:27
  194.8 16.8 %collective-permute-start.19 = (bf16[4,4,32,2048]{3,2,1,0:T(8,128)(2,1)}, bf16[4,4,32,2048]{3,2,1,0:T(8,128)(2,1)}, u32[]{:S(2)}, u32[]{:S(2)}) collective-permute-start(bf16[4,4,32,2048]{3,2,1,0:T(8,128)(2,1)} %dynamic-slice_bitcast_fusion.1), channel_id=1, source_target_pairs={{0,1},{1,0},{2,3},{3,2},{4,5},{5,4},{6,7},{7,6},{8,9},{9,8},{10,11... | collective-permute-start | bytes 6291464 | tf_op jit(solution)/shard_map/ppermute | solution.py:31
  196.3 15.2 %collective-permute-start.18 = (bf16[4,4,64,1024]{3,2,1,0:T(8,128)(2,1)}, bf16[4,4,64,1024]{3,2,1,0:T(8,128)(2,1)}, u32[]{:S(2)}, u32[]{:S(2)}) collective-permute-start(bf16[4,4,64,1024]{3,2,1,0:T(8,128)(2,1)} %dynamic-slice_bitcast_fusion.2), channel_id=1, source_target_pairs={{0,1},{1,0},{2,3},{3,2},{4,5},{5,4},{6,7},{7,6},{8,9},{9,8},{10,11... | collective-permute-start | bytes 6291464 | tf_op jit(solution)/shard_map/ppermute | solution.py:31
  199.0 16.7 %collective-permute-start.22 = (bf16[128,2048]{1,0:T(8,128)(2,1)}, bf16[128,2048]{1,0:T(8,128)(2,1)}, u32[]{:S(2)}, u32[]{:S(2)}) collective-permute-start(bf16[128,2048]{1,0:T(8,128)(2,1)} %fusion.19), channel_id=1, source_target_pairs={{8,0},{16,8},{24,16},{9,1},{17,9},{25,17},{10,2},{18,10},{26,18},{... | collective-permute-start | bytes 1572872 | tf_op jit(solution)/shard_map/ppermute | solution.py:27
  217.8 31.1 %collective-permute-start.23 = (bf16[128,2048]{1,0:T(8,128)(2,1)}, bf16[128,2048]{1,0:T(8,128)(2,1)S(1)}, u32[]{:S(2)}, u32[]{:S(2)}) collective-permute-start(bf16[128,2048]{1,0:T(8,128)(2,1)} %fusion.20), channel_id=1, source_target_pairs={{8,0},{16,8},{24,16},{9,1},{17,9},{25,17},{10,2},{18,10},{26,18},{... | collective-permute-start | bytes 1572872 | tf_op jit(solution)/shard_map/ppermute | solution.py:27
  222.2 26.8 %collective-permute-start.21 = (bf16[4,2,32,2048]{3,2,0,1:T(8,128)(2,1)S(1)}, bf16[4,2,32,2048]{3,2,0,1:T(8,128)(2,1)S(1)}, u32[]{:S(2)}, u32[]{:S(2)}) collective-permute-start(bf16[4,2,32,2048]{3,2,0,1:T(8,128)(2,1)S(1)} %bitcast.147), channel_id=1, source_target_pairs={{0,4},{1,5},{2,6},{3,7},{4,0},{5,1},{6,2},{7,3},{8,12},{9,13},{10,... | collective-permute-start | bytes 3145736 | tf_op jit(solution)/shard_map/ppermute | solution.py:31
  226.2 25.0 %collective-permute-start.20 = (bf16[4,2,64,1024]{3,2,1,0:T(8,128)(2,1)S(1)}, bf16[4,2,64,1024]{3,2,1,0:T(8,128)(2,1)S(1)}, u32[]{:S(2)}, u32[]{:S(2)}) collective-permute-start(bf16[4,2,64,1024]{3,2,1,0:T(8,128)(2,1)S(1)} %dynamic-slice_bitcast_fusion.3), channel_id=1, source_target_pairs={{0,2},{1,3},{2,0},{3,1},{4,6},{5,7},{6,4},{7,5},{8,10},{9,11},{10,... | collective-permute-start | bytes 3145736 | tf_op jit(solution)/shard_map/ppermute | solution.py:31
  276.7 23.1 %collective-permute-start.25 = (bf16[4,32,2048]{2,1,0:T(8,128)(2,1)S(1)}, bf16[4,32,2048]{2,1,0:T(8,128)(2,1)S(1)}, u32[]{:S(2)}, u32[]{:S(2)}) collective-permute-start(bf16[4,32,2048]{2,1,0:T(8,128)(2,1)S(1)} %dynamic-slice_bitcast_fusion.6), channel_id=1, source_target_pairs={{0,2},{1,3},{2,0},{3,1},{4,6},{5,7},{6,4},{7,5},{8,10},{9,11},{10,... | collective-permute-start | bytes 1572872 | tf_op jit(solution)/shard_map/ppermute | solution.py:31
  278.4 21.4 %collective-permute-start.24 = (bf16[4,64,1024]{2,1,0:T(8,128)(2,1)S(1)}, bf16[4,64,1024]{2,1,0:T(8,128)(2,1)S(1)}, u32[]{:S(2)}, u32[]{:S(2)}) collective-permute-start(bf16[4,64,1024]{2,1,0:T(8,128)(2,1)S(1)} %dynamic-slice_bitcast_fusion.7), channel_id=1, source_target_pairs={{0,4},{1,5},{2,6},{3,7},{4,0},{5,1},{6,2},{7,3},{8,12},{9,13},{10,... | collective-permute-start | bytes 1572872 | tf_op jit(solution)/shard_map/ppermute | solution.py:31
  310.7 12.7 %collective-permute-start.30 = (bf16[4,4,32,2432]{3,2,1,0:T(8,128)(2,1)}, bf16[4,4,32,2432]{3,2,1,0:T(8,128)(2,1)}, u32[]{:S(2)}, u32[]{:S(2)}) collective-permute-start(bf16[4,4,32,2432]{3,2,1,0:T(8,128)(2,1)} %dynamic-slice_bitcast_fusion), channel_id=1, source_target_pairs={{0,1},{1,0},{2,3},{3,2},{4,5},{5,4},{6,7},{7,6},{8,9},{9,8},{10,11... | collective-permute-start | bytes 7471112 | tf_op jit(solution)/shard_map/ppermute | solution.py:31
  326.7 21.6 %collective-permute-start.32 = (bf16[4,2,16,2432]{3,2,1,0:T(8,128)(2,1)}, bf16[4,2,16,2432]{3,2,1,0:T(8,128)(2,1)}, u32[]{:S(2)}, u32[]{:S(2)}) collective-permute-start(bf16[4,2,16,2432]{3,2,1,0:T(8,128)(2,1)} %dynamic-slice_bitcast_fusion.4), channel_id=1, source_target_pairs={{0,4},{1,5},{2,6},{3,7},{4,0},{5,1},{6,2},{7,3},{8,12},{9,13},{10,... | collective-permute-start | bytes 1867784 | tf_op jit(solution)/shard_map/ppermute | solution.py:31
  328.7 19.6 %collective-permute-start.31 = (bf16[4,2,16,2432]{3,2,1,0:T(8,128)(2,1)}, bf16[4,2,16,2432]{3,2,1,0:T(8,128)(2,1)}, u32[]{:S(2)}, u32[]{:S(2)}) collective-permute-start(bf16[4,2,16,2432]{3,2,1,0:T(8,128)(2,1)} %dynamic-slice_bitcast_fusion.5), channel_id=1, source_target_pairs={{0,2},{1,3},{2,0},{3,1},{4,6},{5,7},{6,4},{7,5},{8,10},{9,11},{10,... | collective-permute-start | bytes 1867784 | tf_op jit(solution)/shard_map/ppermute | solution.py:31
  336.2 39.5 %collective-permute-start.27 = (bf16[128,1024]{1,0:T(8,128)(2,1)}, bf16[128,1024]{1,0:T(8,128)(2,1)S(1)}, u32[]{:S(2)}, u32[]{:S(2)}) collective-permute-start(bf16[128,1024]{1,0:T(8,128)(2,1)} %get-tuple-element.160), channel_id=1, source_target_pairs={{0,8},{8,16},{16,24},{24,0},{1,9},{9,17},{17,25},{25,1},{2,10},{10... | collective-permute-start | bytes 786440 | tf_op jit(solution)/shard_map/ppermute | solution.py:153
  338.3 37.5 %collective-permute-start.28 = (bf16[128,1024]{1,0:T(8,128)(2,1)}, bf16[128,1024]{1,0:T(8,128)(2,1)}, u32[]{:S(2)}, u32[]{:S(2)}) collective-permute-start(bf16[128,1024]{1,0:T(8,128)(2,1)} %get-tuple-element.161), channel_id=1, source_target_pairs={{0,16},{8,24},{16,0},{24,8},{1,17},{9,25},{17,1},{25,9},{2,18},{10... | collective-permute-start | bytes 786440 | tf_op jit(solution)/shard_map/ppermute | solution.py:153
  345.0 30.7 %collective-permute-start.29 = (bf16[128,1024]{1,0:T(8,128)(2,1)}, bf16[128,1024]{1,0:T(8,128)(2,1)}, u32[]{:S(2)}, u32[]{:S(2)}) collective-permute-start(bf16[128,1024]{1,0:T(8,128)(2,1)} %get-tuple-element.159), channel_id=1, source_target_pairs={{0,24},{8,0},{16,8},{24,16},{1,25},{9,1},{17,9},{25,17},{2,26},{10... | collective-permute-start | bytes 786440 | tf_op jit(solution)/shard_map/ppermute | solution.py:153
  352.1 23.6 %collective-permute-start.36 = (bf16[4,16,2432]{2,1,0:T(8,128)(2,1)}, bf16[4,16,2432]{2,1,0:T(8,128)(2,1)}, u32[]{:S(2)}, u32[]{:S(2)}) collective-permute-start(bf16[4,16,2432]{2,1,0:T(8,128)(2,1)} %dynamic-slice_bitcast_fusion.8), channel_id=1, source_target_pairs={{0,2},{1,3},{2,0},{3,1},{4,6},{5,7},{6,4},{7,5},{8,10},{9,11},{10,... | collective-permute-start | bytes 933896 | tf_op jit(solution)/shard_map/ppermute | solution.py:31
  380.9 12.7 %collective-permute-start.38 = (bf16[32,2432]{1,0:T(8,128)(2,1)S(1)}, bf16[32,2432]{1,0:T(8,128)(2,1)S(1)}, u32[]{:S(2)}, u32[]{:S(2)}) collective-permute-start(bf16[32,2432]{1,0:T(8,128)(2,1)S(1)} %get-tuple-element.164), channel_id=1, source_target_pairs={{0,16},{8,24},{16,0},{24,8},{1,17},{9,25},{17,1},{25,9},{2,18},{10... | collective-permute-start | bytes 466952 | tf_op jit(solution)/shard_map/ppermute | solution.py:153
  (81 other events, 702.5 us)
Sparse Core Ops, SparseCore 0:
  30.0 37.7 all-gather.2
  69.7 36.7 all-gather.4
